TPU v7x, 32 devices: a whole 2x2x4 slice. The times are simulated.
32 devices in a mesh: fsdp: 16 (over z, x, core), pos: 2 (over y).
Axes of the slice: x: 2, y: 2, z: 4, core: 2. Of those that a mesh axis runs over, the one named last changes fastest.
Arguments:
- inputs: bfloat16 [4096, 2, 1024], P('fsdp', 'pos'), may hold values from -6 to 6
- frame_flags: int32 [4096], P('fsdp'), may hold values 0 or 1
- attn_gain: bfloat16 [1, 2, 1024], P(None, 'pos', 'fsdp'), may hold values from 0.25 to 1.75
- qkv_weight: bfloat16 [1, 2, 1024, 3072], P(None, 'pos', 'fsdp'), may hold values from -0.1875 to 0.1875
- out_weight: bfloat16 [1, 2, 1024, 1024], P(None, 'pos', 'fsdp'), may hold values from -0.25 to 0.25
- ffn_gain: bfloat16 [1, 2, 1024], P(None, 'pos', 'fsdp'), may hold values from 0.25 to 1.75
- gate_up_weight: bfloat16 [1, 2, 1024, 8192], P(None, 'pos', 'fsdp'), may hold values from -0.1875 to 0.1875
- down_weight: bfloat16 [1, 2, 4096, 1024], P(None, 'pos', 'fsdp'), may hold values from -0.1875 to 0.1875
- cotangent: bfloat16 [4096, 2, 1024], P('fsdp', 'pos'), may hold values from -6 to 6
Outputs:
- outputs: bfloat16 [4096, 2, 1024], P('fsdp', 'pos')
- input_grad: float32 [4096, 2, 1024], P('fsdp', 'pos')
- attn_gain_grad: float32 [1, 2, 1024], P(None, 'pos', 'fsdp')
- qkv_weight_grad: float32 [1, 2, 1024, 3072], P(None, 'pos', 'fsdp')
- out_weight_grad: float32 [1, 2, 1024, 1024], P(None, 'pos', 'fsdp')
- ffn_gain_grad: float32 [1, 2, 1024], P(None, 'pos', 'fsdp')
- gate_up_weight_grad: float32 [1, 2, 1024, 8192], P(None, 'pos', 'fsdp')
- down_weight_grad: float32 [1, 2, 4096, 1024], P(None, 'pos', 'fsdp')
All inputs are finite; a program needn't handle non-finite values. No bound on the sum of `frame_flags` on one device may be relied on, other than what follows from the above.
Results may differ from a plain program's by a relative error of at most 0.01.
Values may be sent and summed in bfloat16 or wider, within the bound.
A program may use at most 192 MiB of HBM per device.

v0:
```python
import math

import jax
import jax.numpy as jnp
from jax import lax
from jax.sharding import PartitionSpec as P

D = 1024
HEADS = 16
HEAD_DIM = 64
FF = 4096


EPSILON = 1e-06
MASKED = -1e30
PRECISE = lax.Precision.HIGHEST


def rms_parts(hidden, gain_row):
    inv_rms = lax.rsqrt(jnp.mean(hidden * hidden, axis=-1, keepdims=True) + EPSILON)
    return (hidden * inv_rms * gain_row[None], inv_rms)


def rms_back(grad_rows, hidden, inv_rms, gain_row):
    scaled = grad_rows * gain_row[None]
    gain_grad = jnp.sum(grad_rows * hidden * inv_rms, axis=0)
    inner_mean = jnp.mean(scaled * hidden, axis=-1, keepdims=True)
    return (inv_rms * scaled - hidden * inv_rms**3 * inner_mean, gain_grad)


def apply_rows(left_side, weight):
    return jnp.einsum("fpd,pde->fpe", left_side, weight, preferred_element_type=jnp.float32)


def apply_back(grad_rows, weight):
    return jnp.einsum("fpe,pde->fpd", grad_rows, weight, preferred_element_type=jnp.float32)


def outer_sum(left_side, grad_rows):
    return jnp.einsum("fpd,fpe->pde", left_side, grad_rows, preferred_element_type=jnp.float32)


def split_heads(rows):
    return rows.reshape(rows.shape[0], rows.shape[1], HEADS, HEAD_DIM)


def attention_weights(attn_gain, qkv_weight, out_weight, layer_idx):
    return (
        lax.all_gather(attn_gain[layer_idx], "fsdp", axis=1, tiled=True),
        lax.all_gather(qkv_weight[layer_idx], "fsdp", axis=1, tiled=True),
        lax.all_gather(out_weight[layer_idx], "fsdp", axis=1, tiled=True),
    )


def ffn_weights(ffn_gain, gate_up_weight, down_weight, layer_idx):
    return (
        lax.all_gather(ffn_gain[layer_idx], "fsdp", axis=1, tiled=True),
        lax.all_gather(gate_up_weight[layer_idx], "fsdp", axis=1, tiled=True),
        lax.all_gather(down_weight[layer_idx], "fsdp", axis=1, tiled=True),
    )


def attention_forward(qkv_rows):
    frames, places = (qkv_rows.shape[0], qkv_rows.shape[1])
    pos_count = lax.axis_size("pos")
    frame_part = frames // pos_count
    outgoing = qkv_rows.reshape(pos_count, frame_part, places, 3 * D)
    frame_qkv = lax.all_to_all(outgoing, "pos", split_axis=0, concat_axis=2, tiled=True)[0].astype(
        jnp.float32
    )
    whole_places = frame_qkv.shape[1]
    queries = split_heads(frame_qkv[..., :D])
    keys_all = split_heads(frame_qkv[..., D : 2 * D])
    values_all = split_heads(frame_qkv[..., 2 * D :])
    scores = jnp.einsum("fphe,fjhe->fhpj", queries, keys_all, precision=PRECISE) / math.sqrt(
        HEAD_DIM
    )
    causal = jnp.arange(whole_places)[:, None] >= jnp.arange(whole_places)[None, :]
    scores = jnp.where(causal, scores, MASKED)
    row_max = jnp.max(scores, axis=-1, keepdims=True)
    exponent = jnp.exp(scores - row_max)
    attn_probs = exponent / jnp.sum(exponent, axis=-1, keepdims=True)
    mixed_heads = jnp.einsum("fhpj,fjhe->fphe", attn_probs, values_all, precision=PRECISE)
    mixed_frames = mixed_heads.reshape(frame_part, whole_places, D).astype(jnp.bfloat16)
    returned = lax.all_to_all(mixed_frames[None], "pos", split_axis=2, concat_axis=0, tiled=True)
    return (returned.reshape(frames, places, D), (queries, keys_all, values_all, attn_probs))


def attention_backward(grad_mixed, attn_keep):
    queries, keys_all, values_all, attn_probs = attn_keep
    frames, places = (grad_mixed.shape[0], grad_mixed.shape[1])
    pos_count = lax.axis_size("pos")
    frame_part = frames // pos_count
    outgoing = grad_mixed.reshape(pos_count, frame_part, places, D)
    grad_frames = lax.all_to_all(
        outgoing.astype(jnp.bfloat16), "pos", split_axis=0, concat_axis=2, tiled=True
    ).astype(outgoing.dtype)[0]
    whole_places = grad_frames.shape[1]
    grad_heads = split_heads(grad_frames)
    grad_values = jnp.einsum("fhpj,fphe->fjhe", attn_probs, grad_heads, precision=PRECISE)
    grad_probs = jnp.einsum("fphe,fjhe->fhpj", grad_heads, values_all, precision=PRECISE)
    grad_scores = (
        attn_probs
        * (grad_probs - jnp.sum(attn_probs * grad_probs, axis=-1, keepdims=True))
        / math.sqrt(HEAD_DIM)
    )
    grad_queries = jnp.einsum("fhpj,fjhe->fphe", grad_scores, keys_all, precision=PRECISE)
    grad_keys = jnp.einsum("fhpj,fphe->fjhe", grad_scores, queries, precision=PRECISE)
    frame_grads = jnp.concatenate(
        [
            grad_queries.reshape(frame_part, whole_places, D),
            grad_keys.reshape(frame_part, whole_places, D),
            grad_values.reshape(frame_part, whole_places, D),
        ],
        axis=-1,
    ).astype(jnp.bfloat16)
    returned = lax.all_to_all(frame_grads[None], "pos", split_axis=2, concat_axis=0, tiled=True)
    return returned.reshape(frames, places, 3 * D)


def layer_forward(hidden, frame_mask, attn_set, ffn_set):
    gain_one, qkv_full, out_full = attn_set
    gain_two, gate_up_full, down_full = ffn_set
    normed, inv_one = rms_parts(hidden, gain_one.astype(jnp.float32))
    normed_low = normed.astype(jnp.bfloat16)
    qkv_rows = apply_rows(normed_low, qkv_full).astype(jnp.bfloat16)
    mixed_low, attn_keep = attention_forward(qkv_rows)
    hidden_mid = hidden + apply_rows(mixed_low, out_full)
    normed_two, inv_two = rms_parts(hidden_mid, gain_two.astype(jnp.float32))
    normed_two_low = normed_two.astype(jnp.bfloat16)
    gate_up = apply_rows(normed_two_low, gate_up_full)
    gate_part = gate_up[..., :FF]
    up_part = gate_up[..., FF:]
    act_low = (jax.nn.silu(gate_part) * up_part).astype(jnp.bfloat16)
    result = frame_mask * (hidden_mid + apply_rows(act_low, down_full))
    kept_state = (
        hidden,
        inv_one,
        normed_low,
        attn_keep,
        mixed_low,
        hidden_mid,
        inv_two,
        normed_two_low,
        gate_part,
        up_part,
        act_low,
    )
    return (result, kept_state)


def layer_backward(grad_out, frame_mask, kept_state, ffn_set, fetch_attn):
    (
        hidden,
        inv_one,
        normed_low,
        attn_keep,
        mixed_low,
        hidden_mid,
        inv_two,
        normed_two_low,
        gate_part,
        up_part,
        act_low,
    ) = kept_state
    gain_two, gate_up_full, down_full = ffn_set
    grad_sum = frame_mask * grad_out
    grad_ffn = grad_sum.astype(jnp.bfloat16)
    down_grad = outer_sum(act_low, grad_ffn)
    down_shard = lax.psum_scatter(down_grad, "fsdp", scatter_dimension=1, tiled=True)
    grad_act = apply_back(grad_ffn, down_full)
    sigmoid_gate = jax.nn.sigmoid(gate_part)
    grad_gate = grad_act * up_part * sigmoid_gate * (1.0 + gate_part * (1.0 - sigmoid_gate))
    grad_up = grad_act * gate_part * sigmoid_gate
    grad_gu = jnp.concatenate([grad_gate, grad_up], axis=-1).astype(jnp.bfloat16)
    gate_up_grad = outer_sum(normed_two_low, grad_gu)
    grad_norm_two = apply_back(grad_gu, gate_up_full)
    grad_mid_norm, gain_two_grad = rms_back(
        grad_norm_two, hidden_mid, inv_two, gain_two.astype(jnp.float32)
    )
    ffn_shards = (
        lax.psum_scatter(gain_two_grad, "fsdp", scatter_dimension=1, tiled=True),
        lax.psum_scatter(gate_up_grad, "fsdp", scatter_dimension=1, tiled=True),
    )
    gain_one, qkv_full, out_full = fetch_attn()
    grad_mid = grad_sum + grad_mid_norm
    grad_attn = grad_mid.astype(jnp.bfloat16)
    out_grad = outer_sum(mixed_low, grad_attn)
    grad_mixed = apply_back(grad_attn, out_full)
    grad_qkv = attention_backward(grad_mixed, attn_keep)
    qkv_grad = outer_sum(normed_low, grad_qkv)
    grad_norm_one = apply_back(grad_qkv, qkv_full)
    grad_in_norm, gain_one_grad = rms_back(
        grad_norm_one, hidden, inv_one, gain_one.astype(jnp.float32)
    )
    attn_shards = (
        lax.psum_scatter(gain_one_grad, "fsdp", scatter_dimension=1, tiled=True),
        lax.psum_scatter(qkv_grad, "fsdp", scatter_dimension=1, tiled=True),
        lax.psum_scatter(out_grad, "fsdp", scatter_dimension=1, tiled=True),
    )
    grad_in = grad_mid + grad_in_norm
    return (
        grad_in,
        (attn_shards[0], attn_shards[1], attn_shards[2], ffn_shards[0], ffn_shards[1], down_shard),
    )


def on_device(
    inputs,
    frame_flags,
    attn_gain,
    qkv_weight,
    out_weight,
    ffn_gain,
    gate_up_weight,
    down_weight,
    cotangent,
):
    layer_total = qkv_weight.shape[0]
    frame_mask = frame_flags.astype(jnp.float32)[:, None, None]
    hidden = inputs.astype(jnp.float32)
    layer_idx = 0
    attn_set = attention_weights(attn_gain, qkv_weight, out_weight, layer_idx)
    ffn_set = ffn_weights(ffn_gain, gate_up_weight, down_weight, layer_idx)
    hidden, kept_state = layer_forward(hidden, frame_mask, attn_set, ffn_set)
    states_all = [kept_state]
    grad_rows = cotangent.astype(jnp.float32)
    layer_grads = [None] * layer_total
    for layer_idx in reversed(range(layer_total)):
        ffn_set = ffn_weights(ffn_gain, gate_up_weight, down_weight, layer_idx)
        fetch_attn = gather_later(attn_gain, qkv_weight, out_weight, layer_idx)
        grad_rows, layer_grads[layer_idx] = layer_backward(
            grad_rows, frame_mask, states_all[layer_idx], ffn_set, fetch_attn
        )
    stacked = [jnp.stack([grad_set[column] for grad_set in layer_grads]) for column in range(6)]
    return (
        hidden.astype(jnp.bfloat16),
        grad_rows,
        stacked[0],
        stacked[1],
        stacked[2],
        stacked[3],
        stacked[4],
        stacked[5],
    )


def gather_later(attn_gain, qkv_weight, out_weight, layer_idx):

    def fetched():
        return attention_weights(attn_gain, qkv_weight, out_weight, layer_idx)

    return fetched


def solution(mesh):
    in_specs = (
        P("fsdp", "pos", None),
        P("fsdp"),
        P(None, "pos", "fsdp"),
        P(None, "pos", "fsdp", None),
        P(None, "pos", "fsdp", None),
        P(None, "pos", "fsdp"),
        P(None, "pos", "fsdp", None),
        P(None, "pos", "fsdp", None),
        P("fsdp", "pos", None),
    )
    out_specs = (
        P("fsdp", "pos", None),
        P("fsdp", "pos", None),
        P(None, "pos", "fsdp"),
        P(None, "pos", "fsdp", None),
        P(None, "pos", "fsdp", None),
        P(None, "pos", "fsdp"),
        P(None, "pos", "fsdp", None),
        P(None, "pos", "fsdp", None),
    )
    return jax.shard_map(
        on_device, mesh=mesh, in_specs=in_specs, out_specs=out_specs, check_vma=False
    )
```

profile of v0, /device:TPU:0, one launch (start us, length us, event | category | flops | bytes accessed | tf_op | source)
XLA Modules:
  0.0 1286.6 jit_solution(229467966780560589)
XLA Ops:
  11.7 35.2 %all-reduce.2 = (bf16[1024]{0:T(1024)(128)(2,1)S(1)}, bf16[1024]{0:T(1024)(128)(2,1)S(1)}) all-reduce(bf16[1024]{0:T(1024)(128)(2,1)S(1)} %dynamic-update-slice, bf16[1024]{0:T(1024)(128)(2,1)S(1)} %dynamic-update-slice.1), channel_id=2, replica_groups=mesh['fsdp'=16,'pos'=2] {'fsdp'}, use_global_device_ids=true, to_apply=%add | all-reduce | flops 2048 | bytes 8192
  47.1 28.0 %all-gather.11.cloned.1.call-done = bf16[1,1,1024,3072]{3,2,1,0:T(8,128)(2,1)} async-done(((bf16[1,1,64,3072]{3,2,1,0:T(8,128)(2,1)}), bf16[1,1,1024,3072]{3,2,1,0:T(8,128)(2,1)}) %all-gather.11.cloned.1.call-update) | async-done | bytes 6291472 | tf_op jit(solution)/shard_map/all_gather | solution.py:50
  75.1 4.6 fusion.18
  81.3 3.7 all-to-all-start
  85.0 19.9 %all-to-all-done = bf16[2,128,1,3072]{1,3,2,0:T(8,128)(2,1)S(1)} async-done(((bf16[2,128,1,3072]{1,3,2,0:T(8,128)(2,1)}), bf16[2,128,1,3072]{1,3,2,0:T(8,128)(2,1)S(1)}, u32[]{:S(2)}, u32[]{:S(2)}) %all-to-all-start) | async-done | bytes 1572896 | tf_op jit(solution)/shard_map/all_to_all | solution.py:68
  112.4 5.1 fusion.95
  117.5 3.7 fusion.68
  124.9 8.7 fusion.32
  139.2 7.9 all-to-all-done.1
  149.8 95.4 %all-gather.15.cloned.1.call-done = bf16[1,1,1024,8192]{3,2,1,0:T(8,128)(2,1)} async-done(((bf16[1,1,64,8192]{3,2,1,0:T(8,128)(2,1)}), bf16[1,1,1024,8192]{3,2,1,0:T(8,128)(2,1)}) %all-gather.15.cloned.1.call-update) | async-done | bytes 16777232 | tf_op jit(solution)/shard_map/all_gather | solution.py:58
  245.2 12.6 fusion.4
  257.8 62.5 %all-gather.17.cloned.1.call-done = bf16[1,1,4096,1024]{3,2,1,0:T(8,128)(2,1)} async-done(((bf16[1,1,256,1024]{3,2,1,0:T(8,128)(2,1)}), bf16[1,1,4096,1024]{3,2,1,0:T(8,128)(2,1)}) %all-gather.17.cloned.1.call-update) | async-done | bytes 8388624 | tf_op jit(solution)/shard_map/all_gather | solution.py:59
  320.3 13.0 %fusion.28 = (bf16[256,4096]{1,0:T(8,128)(2,1)}, bf16[256,4096]{1,0:T(8,128)(2,1)}, bf16[256,1,4096]{2,0,1:T(8,128)(2,1)}) fusion(f32[256,1,8192]{2,0,1:T(8,128)} %fusion.4, bf16[1,1,4096,1024]{3,2,1,0:T(8,128)(2,1)} %all-gather.17.cloned.1.call-done, bf16[256,1,1024]{2,0,1:T(8,128)(2,1)S(1)} %copy-done.4, f32[256]{0:T(256)S(1)} %convert_element_type.97), kind=kOutput, calls=%fused_computation.41 | convolution fusion | flops 2165047296 | bytes 23593984 | tf_op jit(solution)/shard_map/fpe,pde->fpd/dot_general | solution.py:36
  333.3 12.6 multiply_reduce_fusion.1
  351.6 21.1 %all_to_all.60 = bf16[2,128,1,1024]{1,3,2,0:T(8,128)(2,1)} all-to-all(bf16[2,128,1,1024]{1,3,2,0:T(8,128)(2,1)} %copy.47), channel_id=1, replica_groups=mesh['fsdp'=16,'pos'=2] {'pos'}, dimensions={0} | all-to-all | bytes 1048576 | tf_op jit(solution)/shard_map/all_to_all | solution.py:95
  372.7 3.6 copy.48
  376.3 10.2 fusion.35
  390.1 9.1 fusion.34
  399.2 9.9 fusion.33
  412.7 3.6 copy.52
  422.4 4.6 all-to-all-start.3
  428.2 18.0 %all-to-all-done.3 = bf16[1,128,2,3072]{1,3,0,2:T(8,128)(2,1)} async-done(((bf16[1,128,2,3072]{1,3,0,2:T(8,128)(2,1)}), bf16[1,128,2,3072]{1,3,0,2:T(8,128)(2,1)}, u32[]{:S(2)}, u32[]{:S(2)}) %all-to-all-start.3) | async-done | bytes 1572896 | tf_op jit(solution)/shard_map/all_to_all | solution.py:117
  449.1 6.2 fusion.77
  459.2 7.8 convolution_bitcast_fusion.2
  468.0 9.8 convolution_bitcast_fusion.1
  477.8 15.8 %convolution_bitcast_fusion = f32[1,1024,8192]{2,1,0:T(8,128)} fusion(bf16[256,4096]{1,0:T(8,128)(2,1)} %get-tuple-element.39, bf16[256,4096]{1,0:T(8,128)(2,1)} %get-tuple-element.38, f32[256,1,1024]{2,0,1:T(8,128)S(1)} %get-tuple-element.51, f32[1024]{0:T(1024)S(1)} %mul.221, f32[256]{0:T(256)S(1)} %get-tuple-element.47), kind=kOutput, calls=%fused_computation | convolution fusion | flops 4304142336 | bytes 38802432 | tf_op jit(solution)/shard_map/fpd,fpe->pde/dot_general | solution.py:40
  493.6 7.2 fusion.59
  505.8 38.5 %reduce-scatter.19.cloned.1.call-done = f32[64,1]{1,0:T(8,128)} async-done(((f32[1024,1]{1,0:T(8,128)}), f32[64,1]{1,0:T(8,128)}) %reduce-scatter.19.cloned.1.call-update) | async-done | bytes 272
  545.7 74.6 %reduce-scatter.13.cloned.1.call-done = f32[1,64,1024]{2,1,0:T(8,128)} async-done(((f32[1,1024,1024]{2,1,0:T(8,128)}), f32[1,64,1024]{2,1,0:T(8,128)}) %reduce-scatter.13.cloned.1.call-update) | async-done | bytes 262160 | tf_op jit(solution)/shard_map/reduce_scatter | solution.py:199
  620.3 138.9 %reduce-scatter.11.cloned.1.call-done = f32[1,64,3072]{2,1,0:T(8,128)} async-done(((f32[1,1024,3072]{2,1,0:T(8,128)}), f32[1,64,3072]{2,1,0:T(8,128)}) %reduce-scatter.11.cloned.1.call-update) | async-done | bytes 786448 | tf_op jit(solution)/shard_map/reduce_scatter | solution.py:198
  759.2 183.0 %reduce-scatter.17.cloned.1.call-done = f32[1,256,1024]{2,1,0:T(8,128)} async-done(((f32[1,4096,1024]{2,1,0:T(8,128)}), f32[1,256,1024]{2,1,0:T(8,128)}) %reduce-scatter.17.cloned.1.call-update) | async-done | bytes 1048592 | tf_op jit(solution)/shard_map/reduce_scatter | solution.py:170
  942.2 337.1 %reduce-scatter.15.cloned.1.call-done = f32[1,64,8192]{2,1,0:T(8,128)} async-done(((f32[1,1024,8192]{2,1,0:T(8,128)}), f32[1,64,8192]{2,1,0:T(8,128)}) %reduce-scatter.15.cloned.1.call-update) | async-done | bytes 2097168 | tf_op jit(solution)/shard_map/reduce_scatter | solution.py:183
  (93 shorter events, 58.9 us)
Async XLA Ops:
  7.2 2.8 copy-start.15
  7.2 4.1 copy-start.13
  7.2 4.3 copy-start.14
  7.2 39.8 %copy-start = (bf16[256,1,1024]{2,0,1:T(8,128)(2,1)S(1)}, bf16[256,1,1024]{2,0,1:T(8,128)(2,1)}, u32[]{:S(2)}) copy-start(bf16[256,1,1024]{2,0,1:T(8,128)(2,1)} %param.9) | copy-start | bytes 1572868
  7.2 67.9 %all-gather.11.cloned.1.call-start = ((), (), s32[]{:S(2)}) async-start(), calls=%async_computation.14 | async-start | bytes 6684672 | tf_op jit(solution)/shard_map/all_gather | solution.py:50
  7.9 139.4 %all-gather.13.cloned.1.call-start = ((), (), s32[]{:S(2)}) async-start(), calls=%async_computation.15 | async-start | bytes 2228224 | tf_op jit(solution)/shard_map/all_gather | solution.py:51
  8.7 236.5 %all-gather.15.cloned.1.call-start = ((), (), s32[]{:S(2)}) async-start(), calls=%async_computation.16 | async-start | bytes 17825792 | tf_op jit(solution)/shard_map/all_gather | solution.py:58
  9.4 310.9 %all-gather.17.cloned.1.call-start = ((), (), s32[]{:S(2)}) async-start(), calls=%async_computation.17 | async-start | bytes 8912896 | tf_op jit(solution)/shard_map/all_gather | solution.py:59
  81.3 23.6 %all-to-all-start = ((bf16[2,128,1,3072]{1,3,2,0:T(8,128)(2,1)}), bf16[2,128,1,3072]{1,3,2,0:T(8,128)(2,1)S(1)}, u32[]{:S(2)}, u32[]{:S(2)}) async-start(bf16[2,128,1,3072]{1,3,2,0:T(8,128)(2,1)} %copy.39), calls=%async_computation | async-start | bytes 3145728 | tf_op jit(solution)/shard_map/all_to_all | solution.py:68
  108.3 9.2 copy-start.6
  121.3 3.6 copy-start.9
  123.6 1.3 copy-start.2
  133.7 5.5 copy-start.12
  135.6 11.5 all-to-all-start.1
  245.2 75.1 %copy-start.4 = (bf16[256,1,1024]{2,0,1:T(8,128)(2,1)S(1)}, bf16[256,1,1024]{2,0,1:T(8,128)(2,1)}, u32[]{:S(2)}) copy-start(bf16[256,1,1024]{2,0,1:T(8,128)(2,1)} %param.17) | copy-start | bytes 1572868
  345.9 2.1 copy-start.1
  376.3 10.2 copy-start.3
  376.3 10.2 copy-start.10
  376.3 10.2 copy-start.11
  386.5 3.5 copy-start.7
  390.0 9.1 copy-start.8
  422.4 23.8 %all-to-all-start.3 = ((bf16[1,128,2,3072]{1,3,0,2:T(8,128)(2,1)}), bf16[1,128,2,3072]{1,3,0,2:T(8,128)(2,1)}, u32[]{:S(2)}, u32[]{:S(2)}) async-start(bf16[1,128,2,3072]{1,3,0,2:T(8,128)(2,1)} %maximum_bitcast_fusion), calls=%async_computation.3 | async-start | bytes 3145728 | tf_op jit(solution)/shard_map/all_to_all | solution.py:117
  427.0 73.9 %reduce-scatter.21.cloned.1.call-start = ((), (), s32[]{:S(2)}) async-start(), calls=%async_computation.19 | async-start | bytes 557056
  428.1 116.2 %reduce-scatter.19.cloned.1.call-start = ((), (), s32[]{:S(2)}) async-start(), calls=%async_computation.18 | async-start | bytes 557056
  456.3 164.0 %reduce-scatter.13.cloned.1.call-start = ((), (), s32[]{:S(2)}) async-start(), calls=%async_computation.11 | async-start | bytes 4456448 | tf_op jit(solution)/shard_map/reduce_scatter | solution.py:199
  459.1 300.0 %reduce-scatter.11.cloned.1.call-start = ((), (), s32[]{:S(2)}) async-start(), calls=%async_computation.10 | async-start | bytes 13369344 | tf_op jit(solution)/shard_map/reduce_scatter | solution.py:198
  467.0 1.0 copy-start.5
  467.0 475.2 %reduce-scatter.17.cloned.1.call-start = ((), (), s32[]{:S(2)}) async-start(), calls=%async_computation.13 | async-start | bytes 17825792 | tf_op jit(solution)/shard_map/reduce_scatter | solution.py:170
  477.8 801.5 %reduce-scatter.15.cloned.1.call-start = ((), (), s32[]{:S(2)}) async-start(), calls=%async_computation.12 | async-start | bytes 35651584 | tf_op jit(solution)/shard_map/reduce_scatter | solution.py:183
Sparse Core Ops, SparseCore 0:
  10.3 64.7 all-gather.10
  77.3 40.0 all-gather.12
  119.5 125.6 all-gather.14
  247.2 73.0 all-gather.16
  431.1 54.5 reduce-scatter.20
  489.5 54.7 reduce-scatter.18
  548.8 71.4 reduce-scatter.12
  625.4 133.6 reduce-scatter.10
  764.4 177.7 reduce-scatter.16
  947.5 331.7 reduce-scatter.14
where the time goes:
time: 1300 us; the launch traced here: 1290 us
  waiting for transfers between devices  1010 us (78%)
  matrix products  143 us (11%)
  blocking collectives  56.2 us (4%)
  local copies, waits for them, and re-layouts  40.8 us (3%)
  between operations  15.6 us (1%)
    reduce_scatter x1, waiting for transfers between devices, layer_backward(): lax.psum_scatter(gate_up_grad, 'fsdp', scatter_dimension=1, tiled=True)  337 us
    reduce_scatter x1, waiting for transfers between devices, layer_backward(): lax.psum_scatter(down_grad, 'fsdp', scatter_dimension=1, tiled=True)  183 us
    reduce_scatter x1, waiting for transfers between devices, layer_backward(): lax.psum_scatter(qkv_grad, 'fsdp', scatter_dimension=1, tiled=True)  139 us
    all_gather x1, waiting for transfers between devices, ffn_weights(): lax.all_gather(gate_up_weight[layer_idx], 'fsdp', axis=1, tiled=True)  95.4 us
    reduce_scatter x1, waiting for transfers between devices, layer_backward(): lax.psum_scatter(out_grad, 'fsdp', scatter_dimension=1, tiled=True)  74.6 us
    all_gather x1, waiting for transfers between devices, ffn_weights(): lax.all_gather(down_weight[layer_idx], 'fsdp', axis=1, tiled=True)  62.5 us
    unnamed x12, waiting for transfers between devices  41.2 us
    dot_general x4, matrix products, outer_sum(): jnp.einsum('fpd,fpe->pde', left_side, grad_rows, preferred_element_type=j...  36.1 us
  transfers between devices with their start and end apart: 13, of which 11 were waited for; matrix products, arithmetic and copies ran while one was open for 9% of the time, Pallas kernels for 0%

commit v1 on v0

--- a/solution.py
+++ b/solution.py
@@ -1,8 +1,11 @@
+import functools
 import math
 
 import jax
 import jax.numpy as jnp
 from jax import lax
+from jax.experimental import pallas as pl
+from jax.experimental.pallas import tpu as pltpu
 from jax.sharding import PartitionSpec as P
 
 D = 1024
@@ -253,6 +256,756 @@
     return fetched
 
 
+KEY, VALUE, QUERY, OUT = 0, 1, 2, 3
+SEMS = 128
+MESH = pl.DeviceIdType.MESH
+
+
+def flip(bit, change):
+    return bit + change - 2 * bit * change
+
+
+def square_kernel(
+    x_ref, cot_ref, mask_ref, gain_ref, wqkv, wout, wgu, wd,
+    out_ref, ig_ref, gain_out, gu_out, down_out, attn_out,
+    wa, wgu_all, wd_all, n2_all, g_all, act_all, ggu_all,
+    po_s, po_r, pg_s, pg_r, gu_core, down_core, attn_core, attn_x, attn_z,
+    normed, qb, kb, vb, krem, vrem, mixed, hmid, gv_s, gk_s, gv_r, gk_r,
+    gq, gk, gv, gmid, gattn, hold_k, p_own, p_rem, r_one, r_two,
+    gain_r, gain_f, gsum_s, gsum_r, ends, ends_t,
+    ssem, rsem, lsem, gsem_s, gsem_r, hsem_s, hsem_r,
+):
+    tokens, width = x_ref.shape
+    rows = width // 16
+    block = 4 * width // 4
+    half = block // 2
+    ff = 4 * width
+    f = lax.axis_index("fsdp")
+    y = lax.axis_index("pos")
+    c = f % 2
+    x = (f // 2) % 2
+    z = (f // 4) % 2
+    s = f // 8
+    f32, bf16 = jnp.float32, jnp.bfloat16
+
+    def peer(ds=0, dz=0, dx=0, dc=0):
+        return flip(s, ds) * 8 + flip(z, dz) * 4 + flip(x, dx) * 2 + flip(c, dc)
+
+    def slab(ds=0, dz=0, dx=0, dc=0):
+        return flip(s, ds), flip(z, dz), flip(x, dx), flip(c, dc)
+
+    counter = [0]
+    pending = []
+
+    def take(n=1):
+        counter[0] += n
+        assert counter[0] <= SEMS
+        return counter[0] - n
+
+    def link(src, dst, to, sem=None, to_y=None):
+        if sem is None:
+            sem = take()
+        copy = pltpu.make_async_remote_copy(
+            src_ref=src, dst_ref=dst, send_sem=ssem.at[sem], recv_sem=rsem.at[sem],
+            device_id=(to, y if to_y is None else to_y), device_id_type=MESH,
+        )
+        copy.start()
+        return copy
+
+    lcount = [0]
+
+    def local(src, dst):
+        lcount[0] += 1
+        copy = pltpu.make_async_copy(src, dst, lsem.at[lcount[0] - 1])
+        copy.start()
+        return copy
+
+    def dot(a, b):
+        return jnp.dot(a, b, preferred_element_type=f32)
+
+    def dot_nt(a, b):
+        return lax.dot_general(a, b, (((1,), (1,)), ((), ())), preferred_element_type=f32)
+
+    def split(v):
+        high = v.astype(bf16)
+        return high, (v - high.astype(f32)).astype(bf16)
+
+    def head_sum(v):
+        high, low = split(v)
+        return dot(high, ends[...]) + dot(low, ends[...])
+
+    def head_spread(p):
+        high, low = split(p)
+        return dot(high, ends_t[...]) + dot(low, ends_t[...])
+
+    barrier = pltpu.get_barrier_semaphore()
+
+    @pl.loop(1, 16)
+    def _(r):
+        pl.semaphore_signal(barrier, inc=1, device_id=(lax.rem(f + r, 16), y), device_id_type=MESH)
+
+    pl.semaphore_signal(barrier, inc=1, device_id=(f, 1 - y), device_id_type=MESH)
+    pl.semaphore_wait(barrier, 16)
+
+    def gain_copy(r):
+        return pltpu.make_async_remote_copy(
+            src_ref=gain_ref, dst_ref=gain_r.at[r - 1], send_sem=gsem_s.at[r - 1], recv_sem=gsem_r.at[r - 1],
+            device_id=(lax.rem(f + r, 16), y), device_id_type=MESH,
+        )
+
+    @pl.loop(1, 16)
+    def _(r):
+        gain_copy(r).start()
+
+    own_cols = (
+        wqkv.at[:, pl.ds(width, width)],
+        wqkv.at[:, pl.ds(2 * width, width)],
+        wqkv.at[:, pl.ds(0, width)],
+        wout,
+    )
+    started = {}
+    keep = []
+
+    def gather_start(g):
+        own = wa.at[(g,) + slab()]
+        src = own_cols[g]
+        started[g] = (
+            link(src, own, peer(ds=1)),
+            link(src, own, peer(dz=1)),
+            link(src, own, peer(dx=1)),
+            link(src, own, peer(dc=1)),
+            local(src, own),
+        )
+
+    def forward(g, at, to):
+        ref = wa.at[(g,) + slab(*at)]
+        copy = link(ref, ref, to)
+        keep.append(copy)
+        return copy
+
+    def gather_finish(g):
+        cross, zz, xx, core, own = started[g]
+        keep.extend((cross, zz, xx, core))
+        cross.wait_recv()
+        z_two = forward(g, (1, 0, 0, 0), peer(dz=1))
+        x_two = forward(g, (1, 0, 0, 0), peer(dx=1))
+        cores = [forward(g, (1, 0, 0, 0), peer(dc=1))]
+        zz.wait_recv()
+        x_three = forward(g, (0, 1, 0, 0), peer(dx=1))
+        cores.append(forward(g, (0, 1, 0, 0), peer(dc=1)))
+        z_two.wait_recv()
+        x_four = forward(g, (1, 1, 0, 0), peer(dx=1))
+        cores.append(forward(g, (1, 1, 0, 0), peer(dc=1)))
+        for copy, at in ((xx, (0, 0, 1, 0)), (x_two, (1, 0, 1, 0)), (x_three, (0, 1, 1, 0)), (x_four, (1, 1, 1, 0))):
+            copy.wait_recv()
+            cores.append(forward(g, at, peer(dc=1)))
+        own.wait()
+        core.wait_recv()
+        for copy in cores:
+            copy.wait_recv()
+
+    gather_start(KEY)
+    gather_start(VALUE)
+
+    ends[...] = (
+        lax.broadcasted_iota(jnp.int32, ends.shape, 0) // HEAD_DIM == lax.broadcasted_iota(jnp.int32, ends.shape, 1)
+    ).astype(bf16)
+    ends_t[...] = (
+        lax.broadcasted_iota(jnp.int32, ends_t.shape, 1) // HEAD_DIM == lax.broadcasted_iota(jnp.int32, ends_t.shape, 0)
+    ).astype(bf16)
+
+    g_all[z, x] = (cot_ref[...].astype(f32) * mask_ref[...]).astype(bf16).reshape(2, 2, rows, width)
+
+    gain_f[...] = jnp.zeros_like(gain_f)
+    lane_block = 128
+    per_block = lane_block // rows
+    gain_f[f // per_block] += gain_ref[...].astype(f32)
+
+    @pl.loop(1, 16)
+    def _(r):
+        gain_copy(r).wait()
+        gain_f[lax.rem(f + 16 - r, 16) // per_block] += gain_r[r - 1].astype(f32)
+
+    def gain_row(which):
+        return jnp.concatenate([gain_f[i, which : which + 1, :] for i in range(gain_f.shape[0])], axis=1)
+
+    steps = tokens // rows
+
+    @pl.loop(0, steps)
+    def _(i):
+        part = pl.ds(i * rows, rows)
+        hidden = x_ref[part].astype(f32)
+        inv = lax.rsqrt(jnp.mean(hidden * hidden, axis=-1, keepdims=True) + EPSILON)
+        r_one[part] = jnp.broadcast_to(inv, (rows, 128))
+        normed[part] = (hidden * inv * gain_row(0)).astype(bf16)
+
+    tile = 256 if width >= 256 else width
+    tiles = width // tile
+    quarter = width // 4
+
+    def project(left, g, dest):
+        @pl.loop(0, tiles)
+        def _(t):
+            cols = pl.ds(pl.multiple_of(t * tile, tile), tile)
+            dest[:, cols] = dot(left[...], wa[g, :, :, :, :, :, cols].reshape(width, tile)).astype(dest.dtype)
+
+    gather_finish(KEY)
+    gather_start(QUERY)
+    project(normed, KEY, kb)
+    k_copy = link(kb, krem, f, to_y=1 - y)
+    gather_finish(VALUE)
+    gather_start(OUT)
+    project(normed, VALUE, vb)
+    v_copy = link(vb, vrem, f, to_y=1 - y)
+    gather_finish(QUERY)
+
+    gu_sems = {}
+
+    def gu_pieces(flips):
+        ds, dz, dx = flips
+        j = flip(z, dz) * 2 + flip(x, dx)
+        for u in range(2):
+            for part in range(2):
+                src = wgu.at[:, pl.ds(pl.multiple_of(u * ff + part * (ff // 2) + j * half, half), half)]
+                dst = wgu_all.at[s, z, x, c, :, pl.ds(u * block + part * half, half)]
+                yield src, dst
+
+    order = ((1, 0, 0), (1, 0, 1), (1, 1, 0), (1, 1, 1), (0, 0, 1), (0, 1, 0), (0, 1, 1))
+    for flips in order:
+        sem = take()
+        gu_sems[flips] = sem
+        for src, dst in gu_pieces(flips):
+            link(src, dst, peer(*flips), sem=sem)
+    own_gu_sem = lsem.at[lcount[0]]
+    lcount[0] += 1
+    for src, dst in gu_pieces((0, 0, 0)):
+        pltpu.make_async_copy(src, dst, own_gu_sem).start()
+
+    own_down = wd_all.at[s, c]
+    down_cross = link(wd, own_down, peer(ds=1))
+    down_own_core = link(wd, own_down, peer(dc=1))
+    down_local = local(wd, own_down)
+
+    project(normed, QUERY, qb)
+    gather_finish(OUT)
+
+    g_base = take(3)
+    others = ((0, 1), (1, 0), (1, 1))
+    for i, (dz, dx) in enumerate(others):
+        link(g_all.at[z, x], g_all.at[z, x], peer(0, dz, dx), sem=g_base + i)
+
+    k_copy.wait_recv()
+    v_copy.wait_recv()
+    scale = 1.0 / math.sqrt(HEAD_DIM)
+
+    @pl.loop(0, steps)
+    def _(i):
+        part = pl.ds(i * rows, rows)
+        query = qb[part].astype(f32)
+        own = head_sum(query * kb[part].astype(f32)) * scale
+        far = jnp.where(y > 0, head_sum(query * krem[part].astype(f32)) * scale, MASKED)
+        top = jnp.maximum(own, far)
+        own = jnp.exp(own - top)
+        far = jnp.exp(far - top)
+        total = own + far
+        own = own / total
+        far = far / total
+        p_own[part] = own
+        p_rem[part] = far
+        mixed[part] = (head_spread(own) * vb[part].astype(f32) + head_spread(far) * vrem[part].astype(f32)).astype(bf16)
+
+    project(mixed, OUT, hmid)
+
+    @pl.loop(0, steps)
+    def _(i):
+        part = pl.ds(i * rows, rows)
+        hidden = x_ref[part].astype(f32) + hmid[part]
+        hmid[part] = hidden
+        inv = lax.rsqrt(jnp.mean(hidden * hidden, axis=-1, keepdims=True) + EPSILON)
+        r_two[part] = jnp.broadcast_to(inv, (rows, 128))
+        n2_all[z, x, i // 2, i % 2] = (hidden * inv * gain_row(1)).astype(bf16)
+
+    n2_base = take(3)
+    for i, (dz, dx) in enumerate(others):
+        link(n2_all.at[z, x], n2_all.at[z, x], peer(0, dz, dx), sem=n2_base + i)
+
+    pltpu.make_async_copy(wgu_all.at[slab()], wgu_all.at[slab()], own_gu_sem).wait()
+    gu_cores = []
+    for flips in ((0, 0, 0), (0, 0, 1), (0, 1, 0), (0, 1, 1), (1, 0, 0), (1, 0, 1), (1, 1, 0), (1, 1, 1)):
+        ref = wgu_all.at[slab(*flips)]
+        if flips != (0, 0, 0):
+            pltpu.make_async_copy(ref, ref, rsem.at[gu_sems[flips]]).wait()
+        gu_cores.append(link(ref, ref, peer(dc=1)))
+    down_cross.wait_recv()
+    far_down = wd_all.at[flip(s, 1), c]
+    down_far_core = link(far_down, far_down, peer(dc=1))
+    down_local.wait()
+    down_own_core.wait_recv()
+    down_far_core.wait_recv()
+    for copy in gu_cores:
+        copy.wait_recv()
+
+    po_base = take(3)
+    pg_base = take(3)
+
+    @pl.loop(0, 4)
+    def _(i):
+        dz, dx = i // 2, i % 2
+        cz, cx = flip(z, dz), flip(x, dx)
+        chunk = n2_all.at[cz, cx]
+        g_chunk = g_all.at[cz, cx]
+
+        @pl.when(i > 0)
+        def _():
+            pltpu.make_async_copy(chunk, chunk, rsem.at[n2_base + i - 1]).wait()
+            pltpu.make_async_copy(g_chunk, g_chunk, rsem.at[g_base + i - 1]).wait()
+
+        @pl.loop(0, tiles)
+        def _(t):
+            first = pl.multiple_of(t * tile, tile)
+            cols = pl.ds(first, tile)
+            n2 = chunk[...].reshape(tokens, width)
+            gate = dot(n2, wgu_all[:, :, :, :, :, cols].reshape(width, tile))
+            up = dot(n2, wgu_all[:, :, :, :, :, pl.ds(block + first, tile)].reshape(width, tile))
+            g_act = dot_nt(g_chunk[...].reshape(tokens, width), wd_all[t // 2, t % 2].reshape(tile, width))
+            sig = 1.0 / (1.0 + jnp.exp(-gate))
+            silu = gate * sig
+            shape = (2, 2, rows, tile)
+            act_all[cz, cx, :, :, :, cols] = (silu * up).astype(bf16).reshape(shape)
+            g_gate = g_act * up * sig * (1.0 + gate * (1.0 - sig))
+            ggu_all[cz, cx, :, :, :, cols] = g_gate.astype(bf16).reshape(shape)
+            ggu_all[cz, cx, :, :, :, pl.ds(block + first, tile)] = (g_act * silu).astype(bf16).reshape(shape)
+
+        @pl.loop(0, tiles)
+        def _(t):
+            cols = pl.ds(pl.multiple_of(t * tile, tile), tile)
+            shape = (2, 2, rows, tile)
+            g_n2 = dot_nt(
+                ggu_all[cz, cx].reshape(tokens, 2 * block), wgu_all[t // 2, t % 2].reshape(tile, 2 * block)
+            )
+            pg_s[cz, cx, :, :, :, cols] = g_n2.astype(bf16).reshape(shape)
+
+        @pl.when(i > 0)
+        def _():
+            link(pg_s.at[cz, cx], pg_r.at[i - 1], flip(s, 0) * 8 + cz * 4 + cx * 2 + c, sem=pg_base + i - 1)
+
+        @pl.loop(0, tiles)
+        def _(t):
+            cols = pl.ds(pl.multiple_of(t * tile, tile), tile)
+            shape = (2, 2, rows, tile)
+            part = dot(act_all[cz, cx].reshape(tokens, block), wd_all[:, :, :, :, :, cols].reshape(block, tile))
+            po_s[cz, cx, :, :, :, cols] = part.astype(bf16).reshape(shape)
+
+        @pl.when(i > 0)
+        def _():
+            link(po_s.at[cz, cx], po_r.at[i - 1], flip(s, 0) * 8 + cz * 4 + cx * 2 + c, sem=po_base + i - 1)
+
+    for copy in gu_cores + [down_own_core, down_far_core, down_cross]:
+        copy.wait_send()
+    for i, (dz, dx) in enumerate(others):
+        pltpu.make_async_copy(n2_all.at[z, x], n2_all.at[z, x], ssem.at[n2_base + i]).wait()
+        pltpu.make_async_copy(g_all.at[z, x], g_all.at[z, x], ssem.at[g_base + i]).wait()
+    for flips in order:
+        ref = wgu_all.at[slab(*flips)]
+        pltpu.make_async_copy(ref, ref, ssem.at[gu_sems[flips]]).wait()
+
+    gu_grad = wgu_all
+
+    @pl.loop(0, tiles)
+    def _(t):
+        cols = pl.ds(pl.multiple_of(t * tile, tile), tile)
+        left = n2_all[:, :, :, :, :, cols].reshape(4 * tokens, tile).T
+
+        @pl.loop(0, 2 * block // (2 * tile))
+        def _(n):
+            wide = pl.ds(pl.multiple_of(n * 2 * tile, 2 * tile), 2 * tile)
+            part = dot(left, ggu_all[:, :, :, :, :, wide].reshape(4 * tokens, 2 * tile))
+            gu_grad[t // 2, t % 2, :, :, :, wide] = part.astype(bf16).reshape(2, 2, rows, 2 * tile)
+
+    gu_swap = link(gu_grad.at[:, :, :, flip(c, 1)], gu_core, peer(dc=1))
+
+    down_grad = wd_all
+
+    @pl.loop(0, tiles)
+    def _(t):
+        cols = pl.ds(pl.multiple_of(t * tile, tile), tile)
+        left = act_all[:, :, :, :, :, cols].reshape(4 * tokens, tile).T
+
+        @pl.loop(0, width // (2 * tile))
+        def _(n):
+            wide = pl.ds(pl.multiple_of(n * 2 * tile, 2 * tile), 2 * tile)
+            part = dot(left, g_all[:, :, :, :, :, wide].reshape(4 * tokens, 2 * tile))
+            down_grad[t // 2, t % 2, :, :, :, wide] = part.astype(bf16).reshape(2, 2, rows, 2 * tile)
+
+    down_swap = link(down_grad.at[:, flip(c, 1)], down_core, peer(dc=1))
+
+    gu_swap.wait_recv()
+
+    @pl.loop(0, 8)
+    def _(m):
+        at = (m // 4, (m // 2) % 2, m % 2)
+        ref = gu_grad.at[at + (c,)]
+        ref[...] = (ref[...].astype(f32) + gu_core[at].astype(f32)).astype(bf16)
+
+    gu_sends = []
+    for flips in order:
+        gu_sends.append(link(gu_grad.at[slab(*flips)], gu_out.at[s, z, x], peer(*flips)))
+    gu_keep = local(gu_grad.at[slab()], gu_out.at[s, z, x])
+
+    down_swap.wait_recv()
+
+    @pl.loop(0, 8)
+    def _(m):
+        at = (m // 4,)
+        rest = ((m // 2) % 2, m % 2)
+        ref = down_grad.at[at + (c,) + rest]
+        ref[...] = (ref[...].astype(f32) + down_core[at + rest].astype(f32)).astype(bf16)
+
+    down_send = link(down_grad.at[flip(s, 1), c], down_out.at[1], peer(ds=1))
+    down_keep = local(down_grad.at[s, c], down_out.at[0])
+
+    for i in range(3):
+        pltpu.make_async_copy(pg_r.at[i], pg_r.at[i], rsem.at[pg_base + i]).wait()
+    gsum_s[...] = jnp.zeros_like(gsum_s)
+
+    def add_gain(which, value):
+        for i in range(gsum_s.shape[0]):
+            gsum_s[i, which : which + 1, :] += value[:, i * 128 : (i + 1) * 128]
+
+    @pl.loop(0, steps)
+    def _(i):
+        part = pl.ds(i * rows, rows)
+        at = (i // 2, i % 2)
+        g_n2 = pg_s[(z, x) + at].astype(f32)
+        for k in range(3):
+            g_n2 += pg_r[(k,) + at].astype(f32)
+        hidden = hmid[part]
+        inv = r_two[part][:, :1]
+        add_gain(1, jnp.sum(g_n2 * hidden * inv, axis=0, keepdims=True))
+        scaled = g_n2 * gain_row(1)
+        inner = jnp.mean(scaled * hidden, axis=-1, keepdims=True)
+        g_sum = cot_ref[part].astype(f32) * mask_ref[part]
+        g_mid = g_sum + inv * scaled - hidden * (inv * inv * inv * inner)
+        gmid[part] = g_mid
+        gattn[part] = g_mid.astype(bf16)
+
+    def project_back(left, g, dest):
+        @pl.loop(0, tiles)
+        def _(t):
+            cols = pl.ds(pl.multiple_of(t * tile, tile), tile)
+            dest[:, cols] = dot_nt(left[...], wa[g, t // 2, t % 2].reshape(tile, width))
+
+    g_mixed = ig_ref
+    project_back(gattn, OUT, g_mixed)
+
+    @pl.loop(0, steps)
+    def _(i):
+        part = pl.ds(i * rows, rows)
+        gm = g_mixed[part]
+        gv_s[part] = (head_spread(p_rem[part]) * gm).astype(bf16)
+
+    gv_copy = link(gv_s, gv_r, f, to_y=1 - y)
+
+    @pl.loop(0, steps)
+    def _(i):
+        part = pl.ds(i * rows, rows)
+        gm = g_mixed[part]
+        own, far = p_own[part], p_rem[part]
+        gp_own = head_sum(gm * vb[part].astype(f32))
+        gp_far = head_sum(gm * vrem[part].astype(f32))
+        inner = own * gp_own + far * gp_far
+        gs_own = head_spread(own * (gp_own - inner) * scale)
+        gs_far = head_spread(far * (gp_far - inner) * scale)
+        query = qb[part].astype(f32)
+        gk_s[part] = (gs_far * query).astype(bf16)
+        gq[part] = (gs_own * kb[part].astype(f32) + gs_far * krem[part].astype(f32)).astype(bf16)
+        hold_k[part] = gs_own * query
+
+    gk_copy = link(gk_s, gk_r, f, to_y=1 - y)
+
+    stage = {
+        OUT: (act_all, width),
+        QUERY: (n2_all, width),
+        VALUE: (g_all, width),
+        KEY: (ggu_all, width),
+    }
+    legs = {}
+
+    def grad_view(g, *at):
+        ref = stage[g][0]
+        if ref.shape[-1] != width:
+            return ref.at[at + (slice(None),) * (5 - len(at)) + (pl.ds(0, width),)]
+        return ref.at[at]
+
+    def weight_grad(g, left, right):
+        @pl.loop(0, tiles)
+        def _(t):
+            cols = pl.ds(pl.multiple_of(t * tile, tile), tile)
+            part = dot(left[:, cols].T, right[...])
+            grad_view(g, t // 2, t % 2)[...] = part.astype(bf16).reshape(2, 2, rows, width)
+
+        every = slice(None)
+        legs[g] = [link(grad_view(g, every, every, every, flip(c, 1)), attn_core.at[g], peer(dc=1))]
+
+    def add_into(g, count, at_of, came):
+        @pl.loop(0, count)
+        def _(m):
+            ref = grad_view(g, *at_of(m))
+            ref[...] = (ref[...].astype(f32) + came(m)[...].astype(f32)).astype(bf16)
+
+    def leg_x(g):
+        legs[g][0].wait_recv()
+        add_into(
+            g, 8, lambda m: (m // 4, (m // 2) % 2, m % 2, c), lambda m: attn_core.at[g, m // 4, (m // 2) % 2, m % 2]
+        )
+        every = slice(None)
+        legs[g].append(link(grad_view(g, every, every, flip(x, 1), c), attn_x.at[g], peer(dx=1)))
+
+    def leg_z(g):
+        legs[g][1].wait_recv()
+        add_into(g, 4, lambda m: (m // 2, m % 2, x, c), lambda m: attn_x.at[g, m // 2, m % 2])
+        every = slice(None)
+        legs[g].append(link(grad_view(g, every, flip(z, 1), x, c), attn_z.at[g], peer(dz=1)))
+
+    def leg_cross(g):
+        legs[g][2].wait_recv()
+        add_into(g, 2, lambda m: (m, z, x, c), lambda m: attn_z.at[g, m])
+        legs[g].append(link(grad_view(g, flip(s, 1), z, x, c), attn_out.at[1, g], peer(ds=1)))
+        legs[g].append(local(grad_view(g, s, z, x, c), attn_out.at[0, g]))
+
+    weight_grad(OUT, mixed, gattn)
+    weight_grad(QUERY, normed, gq)
+    leg_x(OUT)
+    leg_x(QUERY)
+    gv_copy.wait_recv()
+
+    @pl.loop(0, steps)
+    def _(i):
+        part = pl.ds(i * rows, rows)
+        own = head_spread(p_own[part]) * g_mixed[part]
+        gv[part] = (own + gv_r[part].astype(f32)).astype(bf16)
+
+    weight_grad(VALUE, normed, gv)
+    leg_x(VALUE)
+    gk_copy.wait_recv()
+
+    @pl.loop(0, steps)
+    def _(i):
+        part = pl.ds(i * rows, rows)
+        gk[part] = (hold_k[part] + gk_r[part].astype(f32)).astype(bf16)
+
+    weight_grad(KEY, normed, gk)
+    leg_z(OUT)
+    leg_x(KEY)
+    leg_z(QUERY)
+    leg_cross(OUT)
+
+    @pl.loop(0, tiles)
+    def _(t):
+        cols = pl.ds(pl.multiple_of(t * tile, tile), tile)
+        at = (t // 2, t % 2)
+        ig_ref[:, cols] = (
+            dot_nt(gq[...], wa[(QUERY,) + at].reshape(tile, width))
+            + dot_nt(gk[...], wa[(KEY,) + at].reshape(tile, width))
+            + dot_nt(gv[...], wa[(VALUE,) + at].reshape(tile, width))
+        )
+
+    @pl.loop(0, steps)
+    def _(i):
+        part = pl.ds(i * rows, rows)
+        hidden = x_ref[part].astype(f32)
+        inv = r_one[part][:, :1]
+        g_n1 = ig_ref[part]
+        add_gain(0, jnp.sum(g_n1 * hidden * inv, axis=0, keepdims=True))
+        scaled = g_n1 * gain_row(0)
+        inner = jnp.mean(scaled * hidden, axis=-1, keepdims=True)
+        ig_ref[part] = gmid[part] + inv * scaled - hidden * (inv * inv * inv * inner)
+
+    def gain_sum_copy(r):
+        to = lax.rem(f + r, 16)
+        return pltpu.make_async_remote_copy(
+            src_ref=gsum_s.at[to // per_block], dst_ref=gsum_r.at[r - 1],
+            send_sem=hsem_s.at[r - 1], recv_sem=hsem_r.at[r - 1],
+            device_id=(to, y), device_id_type=MESH,
+        )
+
+    @pl.loop(1, 16)
+    def _(r):
+        gain_sum_copy(r).start()
+
+    leg_z(VALUE)
+    leg_cross(QUERY)
+    leg_z(KEY)
+    leg_cross(VALUE)
+
+    for i in range(3):
+        pltpu.make_async_copy(po_r.at[i], po_r.at[i], rsem.at[po_base + i]).wait()
+
+    @pl.loop(0, steps)
+    def _(i):
+        part = pl.ds(i * rows, rows)
+        at = (i // 2, i % 2)
+        total = po_s[(z, x) + at].astype(f32)
+        for k in range(3):
+            total += po_r[(k,) + at].astype(f32)
+        out_ref[part] = (mask_ref[part] * (hmid[part] + total)).astype(bf16)
+
+    leg_cross(KEY)
+    gain_out[...] = gsum_s[f // per_block]
+
+    @pl.loop(1, 16)
+    def _(r):
+        gain_sum_copy(r).wait()
+        gain_out[...] += gsum_r[r - 1]
+
+    for copy in keep + [k_copy, v_copy, gv_copy, gk_copy, gu_swap, down_swap]:
+        copy.wait_send()
+    for i in range(3):
+        pltpu.make_async_copy(po_r.at[i], po_r.at[i], ssem.at[po_base + i]).wait()
+        pltpu.make_async_copy(pg_r.at[i], pg_r.at[i], ssem.at[pg_base + i]).wait()
+    for copy in gu_sends + [down_send]:
+        copy.wait()
+    gu_keep.wait()
+    down_keep.wait()
+    for g in (OUT, QUERY, VALUE, KEY):
+        for copy in legs[g][:3]:
+            copy.wait_send()
+        legs[g][3].wait()
+        legs[g][4].wait()
+
+
+def square_layer(inputs, frame_flags, attn_gain, qkv_weight, out_weight, ffn_gain, gate_up_weight, down_weight, cotangent):
+    tokens, _, width = inputs.shape
+    rows = qkv_weight.shape[2]
+    block = width
+    f32, bf16 = jnp.float32, jnp.bfloat16
+    lane_block = 128
+    per_block = lane_block // rows
+    f = lax.axis_index("fsdp")
+    lane_blocks = width // lane_block
+    gains = jnp.concatenate([attn_gain[0], ffn_gain[0]], axis=0)
+    gains = jnp.concatenate([jnp.where(f % per_block == b, gains, 0) for b in range(per_block)], axis=1).astype(bf16)
+    gains = jnp.pad(gains, ((0, 14), (0, 0)))
+    mask = frame_flags.astype(f32)[:, None]
+    vmem = pl.BlockSpec(memory_space=pltpu.VMEM)
+    anywhere = pl.BlockSpec(memory_space=pl.ANY)
+    unit = (2, 2, 2, 2, rows, width)
+    double = (2, 2, 2, 2, rows, 2 * block)
+    own = (tokens, width)
+    scratch = [
+        pltpu.VMEM((4,) + unit, bf16),
+        pltpu.VMEM(double, bf16),
+        pltpu.VMEM(unit, bf16),
+        pltpu.VMEM(unit, bf16),
+        pltpu.VMEM(unit, bf16),
+        pltpu.VMEM(unit, bf16),
+        pltpu.VMEM(double, bf16),
+        pltpu.VMEM(unit, bf16),
+        pltpu.VMEM((3, 2, 2, rows, width), bf16),
+        pltpu.VMEM(unit, bf16),
+        pltpu.VMEM((3, 2, 2, rows, width), bf16),
+        pltpu.VMEM((2, 2, 2, rows, 2 * block), bf16),
+        pltpu.VMEM((2, 2, 2, rows, width), bf16),
+        pltpu.VMEM((4, 2, 2, 2, rows, width), bf16),
+        pltpu.VMEM((4, 2, 2, rows, width), bf16),
+        pltpu.VMEM((4, 2, rows, width), bf16),
+        pltpu.VMEM(own, bf16),
+        pltpu.VMEM(own, bf16),
+        pltpu.VMEM(own, bf16),
+        pltpu.VMEM(own, bf16),
+        pltpu.VMEM(own, bf16),
+        pltpu.VMEM(own, bf16),
+        pltpu.VMEM(own, bf16),
+        pltpu.VMEM(own, f32),
+        pltpu.VMEM(own, bf16),
+        pltpu.VMEM(own, bf16),
+        pltpu.VMEM(own, bf16),
+        pltpu.VMEM(own, bf16),
+        pltpu.VMEM(own, bf16),
+        pltpu.VMEM(own, bf16),
+        pltpu.VMEM(own, bf16),
+        pltpu.VMEM(own, f32),
+        pltpu.VMEM(own, bf16),
+        pltpu.VMEM(own, f32),
+        pltpu.VMEM((tokens, 128), f32),
+        pltpu.VMEM((tokens, 128), f32),
+        pltpu.VMEM((tokens, 128), f32),
+        pltpu.VMEM((tokens, 128), f32),
+        pltpu.VMEM((15, 16, lane_block), bf16),
+        pltpu.VMEM((lane_blocks, 16, lane_block), f32),
+        pltpu.VMEM((lane_blocks, 8, lane_block), f32),
+        pltpu.VMEM((15, 8, lane_block), f32),
+        pltpu.VMEM((width, 128), bf16),
+        pltpu.VMEM((128, width), bf16),
+        pltpu.SemaphoreType.DMA((SEMS,)),
+        pltpu.SemaphoreType.DMA((SEMS,)),
+        pltpu.SemaphoreType.DMA((16,)),
+        pltpu.SemaphoreType.DMA((15,)),
+        pltpu.SemaphoreType.DMA((15,)),
+        pltpu.SemaphoreType.DMA((15,)),
+        pltpu.SemaphoreType.DMA((15,)),
+    ]
+    outs = pl.pallas_call(
+        square_kernel,
+        out_shape=(
+            jax.ShapeDtypeStruct(own, bf16),
+            jax.ShapeDtypeStruct(own, f32),
+            jax.ShapeDtypeStruct((8, lane_block), f32),
+            jax.ShapeDtypeStruct((2, 2, 2, rows, 2 * block), bf16),
+            jax.ShapeDtypeStruct((2, 2, 2, rows, width), bf16),
+            jax.ShapeDtypeStruct((2, 4, rows, width), bf16),
+        ),
+        in_specs=[vmem] * 4 + [anywhere] * 4,
+        out_specs=(vmem, vmem, vmem, anywhere, anywhere, anywhere),
+        scratch_shapes=scratch,
+        compiler_params=pltpu.CompilerParams(
+            collective_id=0, has_side_effects=True, vmem_limit_bytes=VMEM_BYTES
+        ),
+        cost_estimate=pl.CostEstimate(flops=26 * 10**9, bytes_accessed=2**23, transcendentals=2**21),
+    )(
+        inputs[:, 0], cotangent[:, 0], mask, gains,
+        qkv_weight[0, 0], out_weight[0, 0], gate_up_weight[0, 0], down_weight[0, 0].reshape(2, 2, rows, width),
+    )
+    result, input_grad, gain_sums, gu, down, attn = outs
+    gain_sums = sum(
+        jnp.where(f % per_block == b, gain_sums[:2, b * rows : (b + 1) * rows], 0.0) for b in range(per_block)
+    )
+    gu = gu.astype(f32)
+    gu = (gu[0] + gu[1]).reshape(4, rows, 2, 2, block // 2).transpose(1, 2, 3, 0, 4).reshape(1, 1, rows, 8 * block)
+    down = (down[0].astype(f32) + down[1].astype(f32)).reshape(down_weight.shape)
+    attn = attn[0].astype(f32) + attn[1].astype(f32)
+    qkv = jnp.concatenate([attn[QUERY], attn[KEY], attn[VALUE]], axis=1)[None, None]
+    return (
+        result[:, None],
+        input_grad[:, None],
+        gain_sums[0:1, None],
+        qkv,
+        attn[OUT][None, None],
+        gain_sums[1:2, None],
+        gu,
+        down,
+    )
+
+
+VMEM_BYTES = 62 * 2**20
+
+
+def run_layer(axes, *args):
+    inputs, qkv_weight, down_weight = args[0], args[3], args[7]
+    tokens, places, width = inputs.shape
+    rows = qkv_weight.shape[2]
+    square = (
+        axes["fsdp"] == 16
+        and axes["pos"] == 2
+        and places == 1
+        and qkv_weight.shape[0] == 1
+        and tokens == 4 * rows
+        and down_weight.shape[2] == 4 * rows
+        and 128 % rows == 0
+    )
+    return square_layer(*args) if square else on_device(*args)
+
+
 def solution(mesh):
     in_specs = (
         P("fsdp", "pos", None),
@@ -276,5 +1029,5 @@
         P(None, "pos", "fsdp", None),
     )
     return jax.shard_map(
-        on_device, mesh=mesh, in_specs=in_specs, out_specs=out_specs, check_vma=False
-    )
+        functools.partial(run_layer, dict(mesh.shape)), mesh=mesh, in_specs=in_specs, out_specs=out_specs, check_vma=False
+    )

time: 1300 us -> 341 us (0.26)
  waiting for transfers between devices: 1010 us -> 0 us
  Pallas kernels: 0 us -> 320 us
  matrix products: 143 us -> 0 us
  blocking collectives: 56.2 us -> 0 us
  local copies, waits for them, and re-layouts: 40.8 us -> 14.4 us
  between operations: 15.6 us -> 0.71 us
    reduce_scatter x4 -> x0, waiting for transfers between devices: 734 us -> none  [the longest x1 337 us: layer_backward(): lax.psum_scatter(gate_up_grad, 'fsdp', scatter_dimension=1, tiled=True)]
    pallas_call x0 -> x1, Pallas kernels: none -> 320 us  [square_layer(): pl.pallas_call(square_kernel, out_shape=(jax.ShapeDtypeStruct(own, bf16),...]
    all_gather x4 -> x0, waiting for transfers between devices: 186 us -> none  [the longest x1 95.4 us: ffn_weights(): lax.all_gather(gate_up_weight[layer_idx], 'fsdp', axis=1, tiled=True)]
    dot_general x18 -> x0, matrix products: 143 us -> none  [the longest x4 36.1 us: outer_sum(): jnp.einsum('fpd,fpe->pde', left_side, grad_rows, preferred_element_type=j...]
    all_to_all x3 -> x0, waiting for transfers between devices: 45.8 us -> none  [the longest x1 19.9 us: attention_forward(): lax.all_to_all(outgoing, 'pos', split_axis=0, concat_axis=2, tiled=True)[0]]
    unnamed x12 -> x0, waiting for transfers between devices: 41.2 us -> none
    unnamed x1 -> x0, blocking collectives: 35.2 us -> none
    all_to_all x1 -> x0, blocking collectives: 21.1 us -> none  [attention_backward(): lax.all_to_all(outgoing.astype(jnp.bfloat16), 'pos', split_axis=0, concat...]
  transfers between devices with their start and end apart: 13 -> 0, of which waited for: 11 -> 0; matrix products, arithmetic and copies ran while one was open for 9% -> 0% of each run, Pallas kernels for 0% -> 0%
where the time goes in v1:
time: 341 us; the launch traced here: 340 us
  Pallas kernels  320 us (94%)
  local copies, waits for them, and re-layouts  14.4 us (4%)
  other arithmetic  5.9 us (2%)
    pallas_call x1, Pallas kernels, square_layer(): pl.pallas_call(square_kernel, out_shape=(jax.ShapeDtypeStruct(own, bf16),...  320 us

profile of v1, /device:TPU:0, one launch (start us, length us, event | category | flops | bytes accessed | tf_op | source)
XLA Modules:
  0.0 340.5 jit_solution(11695510392472348595)
XLA Ops:
  0.6 0.7 convert_element_type.41
  1.3 0.7 broadcast_select_fusion.1
  2.0 0.7 fusion.2.gain_ref
  2.7 0.8 copy.19.mask_ref
  3.5 319.5 %shard_map.152 = (bf16[256,1024]{1,0:T(8,128)(2,1)}, f32[256,1024]{1,0:T(8,128)}, f32[8,128]{1,0:T(8,128)}, bf16[2,2,2,64,2048]{4,3,2,1,0:T(8,128)(2,1)}, bf16[2...) custom-call(bf16[256,1024]{1,0:T(8,128)(2,1)} %bitcast.35, bf16[256,1024]{1,0:T(8,128)(2,1)} %bitcast.36, ...), custom_call_target="tpu_custom_call" | custom-call | flops 25999998976 | bytes 8388608 | tf_op jit(solution)/shard_map/pallas_call | solution.py:948
  323.0 0.0 copy-start.2
  323.0 0.8 select_add_fusion
  323.8 3.3 copy.21
  327.1 0.5 slice_bitcast_fusion.3
  327.6 0.0 copy-done.2
  327.6 0.2 convert_add_fusion.1
  327.8 0.0 copy-start.1
  327.8 0.8 fusion.3
  328.6 0.0 copy-start
  328.6 0.9 maximum_bitcast_fusion
  329.6 0.0 copy-done.1
  329.6 1.1 convert_add_fusion
  330.7 0.0 copy-done
  330.7 0.5 convert_element_type.44
  331.3 0.3 slice_add_fusion
  331.5 2.8 add.40
  334.3 2.9 copy.20
  337.2 0.0 copy-start.3
  337.3 2.4 reshape.61
  339.7 0.0 copy-done.3
  339.7 0.8 copy.23
Async XLA Ops:
  323.0 4.6 %copy-start.2 = (bf16[2,4,64,1024]{3,2,1,0:T(8,128)(2,1)S(1)}, bf16[2,4,64,1024]{3,2,1,0:T(8,128)(2,1)}, u32[]{:S(2)}) copy-start(bf16[2,4,64,1024]{3,2,1,0:T(8,128)(2,1)} %get-tuple-element.17) | copy-start | bytes 3145732
  327.8 1.8 copy-start.1
  328.6 2.1 copy-start
  337.2 2.5 copy-start.3

commit v2 on v1

--- a/solution.py
+++ b/solution.py
@@ -363,19 +363,20 @@
         wqkv.at[:, pl.ds(0, width)],
         wout,
     )
-    started = {}
     keep = []
-
-    def gather_start(g):
+    legs_in = {g: {} for g in range(4)}
+
+    def own_send(g, *ways):
         own = wa.at[(g,) + slab()]
         src = own_cols[g]
-        started[g] = (
-            link(src, own, peer(ds=1)),
-            link(src, own, peer(dz=1)),
-            link(src, own, peer(dx=1)),
-            link(src, own, peer(dc=1)),
-            local(src, own),
-        )
+        flips = {"s": (1, 0, 0, 0), "z": (0, 1, 0, 0), "x": (0, 0, 1, 0), "c": (0, 0, 0, 1)}
+        for way in ways:
+            copy = link(src, own, peer(*flips[way]))
+            keep.append(copy)
+            legs_in[g][way] = copy
+        if "c" in ways:
+            legs_in[g]["own"] = local(src, own)
+            legs_in[g]["cores"] = []
 
     def forward(g, at, to):
         ref = wa.at[(g,) + slab(*at)]
@@ -383,81 +384,40 @@
         keep.append(copy)
         return copy
 
-    def gather_finish(g):
-        cross, zz, xx, core, own = started[g]
-        keep.extend((cross, zz, xx, core))
-        cross.wait_recv()
-        z_two = forward(g, (1, 0, 0, 0), peer(dz=1))
-        x_two = forward(g, (1, 0, 0, 0), peer(dx=1))
-        cores = [forward(g, (1, 0, 0, 0), peer(dc=1))]
-        zz.wait_recv()
-        x_three = forward(g, (0, 1, 0, 0), peer(dx=1))
-        cores.append(forward(g, (0, 1, 0, 0), peer(dc=1)))
-        z_two.wait_recv()
-        x_four = forward(g, (1, 1, 0, 0), peer(dx=1))
-        cores.append(forward(g, (1, 1, 0, 0), peer(dc=1)))
-        for copy, at in ((xx, (0, 0, 1, 0)), (x_two, (1, 0, 1, 0)), (x_three, (0, 1, 1, 0)), (x_four, (1, 1, 1, 0))):
+    def to_core(g, at):
+        legs_in[g]["cores"].append(forward(g, at, peer(dc=1)))
+
+    def from_cross(g):
+        leg = legs_in[g]
+        leg["s"].wait_recv()
+        leg["sz"] = forward(g, (1, 0, 0, 0), peer(dz=1))
+        leg["sx"] = forward(g, (1, 0, 0, 0), peer(dx=1))
+        to_core(g, (1, 0, 0, 0))
+
+    def from_z(g):
+        leg = legs_in[g]
+        leg["z"].wait_recv()
+        leg["zx"] = forward(g, (0, 1, 0, 0), peer(dx=1))
+        to_core(g, (0, 1, 0, 0))
+
+    def from_cross_z(g):
+        leg = legs_in[g]
+        leg["sz"].wait_recv()
+        leg["szx"] = forward(g, (1, 1, 0, 0), peer(dx=1))
+        to_core(g, (1, 1, 0, 0))
+
+    def from_x(g):
+        leg = legs_in[g]
+        for name, at in (("x", (0, 0, 1, 0)), ("sx", (1, 0, 1, 0)), ("zx", (0, 1, 1, 0)), ("szx", (1, 1, 1, 0))):
+            leg[name].wait_recv()
+            to_core(g, at)
+
+    def from_core(g):
+        leg = legs_in[g]
+        leg["own"].wait()
+        leg["c"].wait_recv()
+        for copy in leg["cores"]:
             copy.wait_recv()
-            cores.append(forward(g, at, peer(dc=1)))
-        own.wait()
-        core.wait_recv()
-        for copy in cores:
-            copy.wait_recv()
-
-    gather_start(KEY)
-    gather_start(VALUE)
-
-    ends[...] = (
-        lax.broadcasted_iota(jnp.int32, ends.shape, 0) // HEAD_DIM == lax.broadcasted_iota(jnp.int32, ends.shape, 1)
-    ).astype(bf16)
-    ends_t[...] = (
-        lax.broadcasted_iota(jnp.int32, ends_t.shape, 1) // HEAD_DIM == lax.broadcasted_iota(jnp.int32, ends_t.shape, 0)
-    ).astype(bf16)
-
-    g_all[z, x] = (cot_ref[...].astype(f32) * mask_ref[...]).astype(bf16).reshape(2, 2, rows, width)
-
-    gain_f[...] = jnp.zeros_like(gain_f)
-    lane_block = 128
-    per_block = lane_block // rows
-    gain_f[f // per_block] += gain_ref[...].astype(f32)
-
-    @pl.loop(1, 16)
-    def _(r):
-        gain_copy(r).wait()
-        gain_f[lax.rem(f + 16 - r, 16) // per_block] += gain_r[r - 1].astype(f32)
-
-    def gain_row(which):
-        return jnp.concatenate([gain_f[i, which : which + 1, :] for i in range(gain_f.shape[0])], axis=1)
-
-    steps = tokens // rows
-
-    @pl.loop(0, steps)
-    def _(i):
-        part = pl.ds(i * rows, rows)
-        hidden = x_ref[part].astype(f32)
-        inv = lax.rsqrt(jnp.mean(hidden * hidden, axis=-1, keepdims=True) + EPSILON)
-        r_one[part] = jnp.broadcast_to(inv, (rows, 128))
-        normed[part] = (hidden * inv * gain_row(0)).astype(bf16)
-
-    tile = 256 if width >= 256 else width
-    tiles = width // tile
-    quarter = width // 4
-
-    def project(left, g, dest):
-        @pl.loop(0, tiles)
-        def _(t):
-            cols = pl.ds(pl.multiple_of(t * tile, tile), tile)
-            dest[:, cols] = dot(left[...], wa[g, :, :, :, :, :, cols].reshape(width, tile)).astype(dest.dtype)
-
-    gather_finish(KEY)
-    gather_start(QUERY)
-    project(normed, KEY, kb)
-    k_copy = link(kb, krem, f, to_y=1 - y)
-    gather_finish(VALUE)
-    gather_start(OUT)
-    project(normed, VALUE, vb)
-    v_copy = link(vb, vrem, f, to_y=1 - y)
-    gather_finish(QUERY)
 
     gu_sems = {}
 
@@ -471,11 +431,91 @@
                 yield src, dst
 
     order = ((1, 0, 0), (1, 0, 1), (1, 1, 0), (1, 1, 1), (0, 0, 1), (0, 1, 0), (0, 1, 1))
-    for flips in order:
+
+    def gu_send(k):
         sem = take()
-        gu_sems[flips] = sem
-        for src, dst in gu_pieces(flips):
-            link(src, dst, peer(*flips), sem=sem)
+        gu_sems[order[k]] = sem
+        for src, dst in gu_pieces(order[k]):
+            link(src, dst, peer(*order[k]), sem=sem)
+
+    own_send(KEY, "s", "z", "x", "c")
+    own_send(VALUE, "s", "z", "x", "c")
+    own_send(QUERY, "x")
+
+    ends[...] = (
+        lax.broadcasted_iota(jnp.int32, ends.shape, 0) // HEAD_DIM == lax.broadcasted_iota(jnp.int32, ends.shape, 1)
+    ).astype(bf16)
+    ends_t[...] = (
+        lax.broadcasted_iota(jnp.int32, ends_t.shape, 1) // HEAD_DIM == lax.broadcasted_iota(jnp.int32, ends_t.shape, 0)
+    ).astype(bf16)
+
+    g_all[z, x] = (cot_ref[...].astype(f32) * mask_ref[...]).astype(bf16).reshape(2, 2, rows, width)
+
+    g_z = link(g_all.at[z, x], g_all.at[z, x], peer(dz=1))
+    g_x = link(g_all.at[z, x], g_all.at[z, x], peer(dx=1))
+
+    gain_f[...] = jnp.zeros_like(gain_f)
+    lane_block = 128
+    per_block = lane_block // rows
+    gain_f[f // per_block] += gain_ref[...].astype(f32)
+
+    @pl.loop(1, 16)
+    def _(r):
+        gain_copy(r).wait()
+        gain_f[lax.rem(f + 16 - r, 16) // per_block] += gain_r[r - 1].astype(f32)
+
+    def gain_row(which):
+        return jnp.concatenate([gain_f[i, which : which + 1, :] for i in range(gain_f.shape[0])], axis=1)
+
+    steps = tokens // rows
+
+    @pl.loop(0, steps)
+    def _(i):
+        part = pl.ds(i * rows, rows)
+        hidden = x_ref[part].astype(f32)
+        inv = lax.rsqrt(jnp.mean(hidden * hidden, axis=-1, keepdims=True) + EPSILON)
+        r_one[part] = jnp.broadcast_to(inv, (rows, 128))
+        normed[part] = (hidden * inv * gain_row(0)).astype(bf16)
+
+    tile = 256 if width >= 256 else width
+    tiles = width // tile
+    quarter = width // 4
+
+    def project(left, g, dest):
+        @pl.loop(0, tiles)
+        def _(t):
+            cols = pl.ds(pl.multiple_of(t * tile, tile), tile)
+            dest[:, cols] = dot(left[...], wa[g, :, :, :, :, :, cols].reshape(width, tile)).astype(dest.dtype)
+
+    from_cross(KEY)
+    from_z(KEY)
+    own_send(QUERY, "s", "z", "c")
+    from_cross(VALUE)
+    from_cross_z(KEY)
+    from_z(VALUE)
+    gu_send(0)
+    own_send(OUT, "x", "s", "z", "c")
+    from_cross(QUERY)
+    from_x(KEY)
+    from_cross_z(VALUE)
+    from_z(QUERY)
+    from_core(KEY)
+    project(normed, KEY, kb)
+    k_copy = link(kb, krem, f, to_y=1 - y)
+    gu_send(1)
+    from_x(VALUE)
+    from_cross_z(QUERY)
+    from_cross(OUT)
+    from_z(OUT)
+    from_core(VALUE)
+    project(normed, VALUE, vb)
+    v_copy = link(vb, vrem, f, to_y=1 - y)
+    gu_send(2)
+    from_cross_z(OUT)
+    gu_send(3)
+    gu_send(6)
+    gu_send(5)
+    gu_send(4)
     own_gu_sem = lsem.at[lcount[0]]
     lcount[0] += 1
     for src, dst in gu_pieces((0, 0, 0)):
@@ -486,13 +526,13 @@
     down_own_core = link(wd, own_down, peer(dc=1))
     down_local = local(wd, own_down)
 
+    from_x(QUERY)
+    g_z.wait_recv()
+    g_zx = link(g_all.at[flip(z, 1), x], g_all.at[flip(z, 1), x], peer(dx=1))
+    from_core(QUERY)
     project(normed, QUERY, qb)
-    gather_finish(OUT)
-
-    g_base = take(3)
-    others = ((0, 1), (1, 0), (1, 1))
-    for i, (dz, dx) in enumerate(others):
-        link(g_all.at[z, x], g_all.at[z, x], peer(0, dz, dx), sem=g_base + i)
+    from_x(OUT)
+    from_core(OUT)
 
     k_copy.wait_recv()
     v_copy.wait_recv()
@@ -525,9 +565,11 @@
         r_two[part] = jnp.broadcast_to(inv, (rows, 128))
         n2_all[z, x, i // 2, i % 2] = (hidden * inv * gain_row(1)).astype(bf16)
 
-    n2_base = take(3)
-    for i, (dz, dx) in enumerate(others):
-        link(n2_all.at[z, x], n2_all.at[z, x], peer(0, dz, dx), sem=n2_base + i)
+    n2_z = link(n2_all.at[z, x], n2_all.at[z, x], peer(dz=1))
+    n2_x = link(n2_all.at[z, x], n2_all.at[z, x], peer(dx=1))
+    n2_zx_sem = take()
+    g_x.wait_recv()
+    g_zx.wait_recv()
 
     pltpu.make_async_copy(wgu_all.at[slab()], wgu_all.at[slab()], own_gu_sem).wait()
     gu_cores = []
@@ -555,10 +597,15 @@
         chunk = n2_all.at[cz, cx]
         g_chunk = g_all.at[cz, cx]
 
-        @pl.when(i > 0)
+        @pl.when(i == 1)
         def _():
-            pltpu.make_async_copy(chunk, chunk, rsem.at[n2_base + i - 1]).wait()
-            pltpu.make_async_copy(g_chunk, g_chunk, rsem.at[g_base + i - 1]).wait()
+            n2_x.wait_recv()
+            n2_z.wait_recv()
+            link(n2_all.at[flip(z, 1), x], n2_all.at[flip(z, 1), x], peer(dx=1), sem=n2_zx_sem)
+
+        @pl.when(i == 3)
+        def _():
+            pltpu.make_async_copy(chunk, chunk, rsem.at[n2_zx_sem]).wait()
 
         @pl.loop(0, tiles)
         def _(t):
@@ -585,9 +632,9 @@
             )
             pg_s[cz, cx, :, :, :, cols] = g_n2.astype(bf16).reshape(shape)
 
-        @pl.when(i > 0)
+        @pl.when(dx == 1)
         def _():
-            link(pg_s.at[cz, cx], pg_r.at[i - 1], flip(s, 0) * 8 + cz * 4 + cx * 2 + c, sem=pg_base + i - 1)
+            link(pg_s.at[cz, cx], pg_r.at[dz], peer(dx=1), sem=pg_base + dz)
 
         @pl.loop(0, tiles)
         def _(t):
@@ -596,15 +643,15 @@
             part = dot(act_all[cz, cx].reshape(tokens, block), wd_all[:, :, :, :, :, cols].reshape(block, tile))
             po_s[cz, cx, :, :, :, cols] = part.astype(bf16).reshape(shape)
 
-        @pl.when(i > 0)
+        @pl.when(dx == 1)
         def _():
-            link(po_s.at[cz, cx], po_r.at[i - 1], flip(s, 0) * 8 + cz * 4 + cx * 2 + c, sem=po_base + i - 1)
+            link(po_s.at[cz, cx], po_r.at[dz], peer(dx=1), sem=po_base + dz)
 
     for copy in gu_cores + [down_own_core, down_far_core, down_cross]:
         copy.wait_send()
-    for i, (dz, dx) in enumerate(others):
-        pltpu.make_async_copy(n2_all.at[z, x], n2_all.at[z, x], ssem.at[n2_base + i]).wait()
-        pltpu.make_async_copy(g_all.at[z, x], g_all.at[z, x], ssem.at[g_base + i]).wait()
+    for copy in (n2_z, n2_x, g_z, g_x, g_zx):
+        copy.wait_send()
+    pltpu.make_async_copy(n2_all.at[z, x], n2_all.at[z, x], ssem.at[n2_zx_sem]).wait()
     for flips in order:
         ref = wgu_all.at[slab(*flips)]
         pltpu.make_async_copy(ref, ref, ssem.at[gu_sems[flips]]).wait()
@@ -623,6 +670,22 @@
             gu_grad[t // 2, t % 2, :, :, :, wide] = part.astype(bf16).reshape(2, 2, rows, 2 * tile)
 
     gu_swap = link(gu_grad.at[:, :, :, flip(c, 1)], gu_core, peer(dc=1))
+
+    def wait_block(block_ref, sem):
+        pltpu.make_async_copy(block_ref, block_ref, sem).wait()
+
+    def partial_z(sent, came, base):
+        wait_block(came.at[1], rsem.at[base + 1])
+
+        @pl.loop(0, 4)
+        def _(m):
+            at = (m // 2, m % 2)
+            ref = sent.at[(flip(z, 1), x) + at]
+            ref[...] = (ref[...].astype(f32) + came[(1,) + at].astype(f32)).astype(bf16)
+
+        return link(sent.at[flip(z, 1), x], came.at[2], peer(dz=1), sem=base + 2)
+
+    partial_z(pg_s, pg_r, pg_base)
 
     down_grad = wd_all
 
@@ -664,8 +727,10 @@
     down_send = link(down_grad.at[flip(s, 1), c], down_out.at[1], peer(ds=1))
     down_keep = local(down_grad.at[s, c], down_out.at[0])
 
-    for i in range(3):
-        pltpu.make_async_copy(pg_r.at[i], pg_r.at[i], rsem.at[pg_base + i]).wait()
+    partial_z(po_s, po_r, po_base)
+
+    for i in (0, 2):
+        wait_block(pg_r.at[i], rsem.at[pg_base + i])
     gsum_s[...] = jnp.zeros_like(gsum_s)
 
     def add_gain(which, value):
@@ -677,7 +742,7 @@
         part = pl.ds(i * rows, rows)
         at = (i // 2, i % 2)
         g_n2 = pg_s[(z, x) + at].astype(f32)
-        for k in range(3):
+        for k in (0, 2):
             g_n2 += pg_r[(k,) + at].astype(f32)
         hidden = hmid[part]
         inv = r_two[part][:, :1]
@@ -838,15 +903,15 @@
     leg_z(KEY)
     leg_cross(VALUE)
 
-    for i in range(3):
-        pltpu.make_async_copy(po_r.at[i], po_r.at[i], rsem.at[po_base + i]).wait()
+    for i in (0, 2):
+        wait_block(po_r.at[i], rsem.at[po_base + i])
 
     @pl.loop(0, steps)
     def _(i):
         part = pl.ds(i * rows, rows)
         at = (i // 2, i % 2)
         total = po_s[(z, x) + at].astype(f32)
-        for k in range(3):
+        for k in (0, 2):
             total += po_r[(k,) + at].astype(f32)
         out_ref[part] = (mask_ref[part] * (hmid[part] + total)).astype(bf16)
 
@@ -861,8 +926,8 @@
     for copy in keep + [k_copy, v_copy, gv_copy, gk_copy, gu_swap, down_swap]:
         copy.wait_send()
     for i in range(3):
-        pltpu.make_async_copy(po_r.at[i], po_r.at[i], ssem.at[po_base + i]).wait()
-        pltpu.make_async_copy(pg_r.at[i], pg_r.at[i], ssem.at[pg_base + i]).wait()
+        wait_block(po_r.at[i], ssem.at[po_base + i])
+        wait_block(pg_r.at[i], ssem.at[pg_base + i])
     for copy in gu_sends + [down_send]:
         copy.wait()
     gu_keep.wait()

time: 341 us -> 303 us (0.89)
  Pallas kernels: 320 us -> 282 us
    pallas_call x1, Pallas kernels: 320 us -> 282 us  [square_layer(): pl.pallas_call(square_kernel, out_shape=(jax.ShapeDtypeStruct(own, bf16),...]
where the time goes in v2:
time: 303 us
  Pallas kernels  282 us (93%)
  local copies, waits for them, and re-layouts  14.4 us (5%)
  other arithmetic  5.9 us (2%)
    pallas_call x1, Pallas kernels, square_layer(): pl.pallas_call(square_kernel, out_shape=(jax.ShapeDtypeStruct(own, bf16),...  282 us

profile of v2, /device:TPU:0, one launch (start us, length us, event | category | flops | bytes accessed | tf_op | source)
XLA Modules:
  0.0 303.1 jit_solution(6905089914476076687)
XLA Ops:
  0.6 0.7 convert_element_type.41
  1.3 0.7 broadcast_select_fusion.1
  2.0 0.7 fusion.2.gain_ref
  2.7 0.8 copy.19.mask_ref
  3.5 282.1 %shard_map.152 = (bf16[256,1024]{1,0:T(8,128)(2,1)}, f32[256,1024]{1,0:T(8,128)}, f32[8,128]{1,0:T(8,128)}, bf16[2,2,2,64,2048]{4,3,2,1,0:T(8,128)(2,1)}, bf16[2...) custom-call(bf16[256,1024]{1,0:T(8,128)(2,1)} %bitcast.35, bf16[256,1024]{1,0:T(8,128)(2,1)} %bitcast.36, ...), custom_call_target="tpu_custom_call" | custom-call | flops 25999998976 | bytes 8388608 | tf_op jit(solution)/shard_map/pallas_call | solution.py:1013
  285.6 0.0 copy-start.2
  285.6 0.8 select_add_fusion
  286.4 3.3 %copy.21 = f32[256,1,1024]{2,1,0:T(1,128)} copy(f32[256,1,1024]{2,0,1:T(8,128)} %bitcast.29) | data formatting | bytes 2097152
  289.7 0.5 slice_bitcast_fusion.3
  290.2 0.0 copy-done.2
  290.2 0.2 convert_add_fusion.1
  290.4 0.0 copy-start.1
  290.4 0.8 fusion.3
  291.2 0.0 copy-start
  291.2 0.9 maximum_bitcast_fusion
  292.1 0.0 copy-done.1
  292.1 1.1 convert_add_fusion
  293.3 0.0 copy-done
  293.3 0.5 convert_element_type.44
  293.8 0.3 slice_add_fusion
  294.1 2.8 add.40
  296.9 2.9 copy.20
  299.8 0.0 copy-start.3
  299.8 2.4 reshape.61
  302.3 0.0 copy-done.3
  302.3 0.8 copy.23
Async XLA Ops:
  285.6 4.6 %copy-start.2 = (bf16[2,4,64,1024]{3,2,1,0:T(8,128)(2,1)S(1)}, bf16[2,4,64,1024]{3,2,1,0:T(8,128)(2,1)}, u32[]{:S(2)}) copy-start(bf16[2,4,64,1024]{3,2,1,0:T(8,128)(2,1)} %get-tuple-element.17) | copy-start | bytes 3145732
  290.4 1.8 copy-start.1
  291.2 2.1 copy-start
  299.8 2.5 copy-start.3

commit v3 on v2

--- a/solution.py
+++ b/solution.py
@@ -266,12 +266,12 @@
 
 
 def square_kernel(
-    x_ref, cot_ref, mask_ref, gain_ref, wqkv, wout, wgu, wd,
-    out_ref, ig_ref, gain_out, gu_out, down_out, attn_out,
+    x_ref, cot_ref, flags_ref, gain_one_ref, gain_two_ref, wqkv, wout, wgu, wd,
+    out_ref, ig_ref, gain_one_out, gain_two_out, gu_out, down_out, attn_out,
     wa, wgu_all, wd_all, n2_all, g_all, act_all, ggu_all,
     po_s, po_r, pg_s, pg_r, gu_core, down_core, attn_core, attn_x, attn_z,
     normed, qb, kb, vb, krem, vrem, mixed, hmid, gv_s, gk_s, gv_r, gk_r,
-    gq, gk, gv, gmid, gattn, hold_k, p_own, p_rem, r_one, r_two,
+    gq, gk, gv, gmid, gattn, hold_k, gwide, mask, gain_ref, p_own, p_rem, r_one, r_two,
     gain_r, gain_f, gsum_s, gsum_r, ends, ends_t,
     ssem, rsem, lsem, gsem_s, gsem_r, hsem_s, hsem_r,
 ):
@@ -347,6 +347,17 @@
     pl.semaphore_signal(barrier, inc=1, device_id=(f, 1 - y), device_id_type=MESH)
     pl.semaphore_wait(barrier, 16)
 
+    lane_block = 128
+    per_block = lane_block // rows
+    lanes = lax.broadcasted_iota(jnp.int32, gain_ref.shape, 1) // rows == f % per_block
+    sublane = lax.broadcasted_iota(jnp.int32, gain_ref.shape, 0)
+
+    def lane_tile(ref):
+        return jnp.concatenate([ref[...].astype(f32)] * per_block, axis=1)
+
+    gains = jnp.where(sublane == 0, lane_tile(gain_one_ref), jnp.where(sublane == 1, lane_tile(gain_two_ref), 0.0))
+    gain_ref[...] = jnp.where(lanes, gains, 0.0).astype(bf16)
+
     def gain_copy(r):
         return pltpu.make_async_remote_copy(
             src_ref=gain_ref, dst_ref=gain_r.at[r - 1], send_sem=gsem_s.at[r - 1], recv_sem=gsem_r.at[r - 1],
@@ -449,14 +460,15 @@
         lax.broadcasted_iota(jnp.int32, ends_t.shape, 1) // HEAD_DIM == lax.broadcasted_iota(jnp.int32, ends_t.shape, 0)
     ).astype(bf16)
 
-    g_all[z, x] = (cot_ref[...].astype(f32) * mask_ref[...]).astype(bf16).reshape(2, 2, rows, width)
+    for i in range(tokens // 128):
+        flags = flags_ref[i : i + 1, :].astype(f32)
+        mask[i * 128 : (i + 1) * 128] = jnp.broadcast_to(flags, (128, 128)).T
+    g_all[z, x] = (cot_ref[...].astype(f32) * mask[:, :1]).astype(bf16).reshape(2, 2, rows, width)
 
     g_z = link(g_all.at[z, x], g_all.at[z, x], peer(dz=1))
     g_x = link(g_all.at[z, x], g_all.at[z, x], peer(dx=1))
 
     gain_f[...] = jnp.zeros_like(gain_f)
-    lane_block = 128
-    per_block = lane_block // rows
     gain_f[f // per_block] += gain_ref[...].astype(f32)
 
     @pl.loop(1, 16)
@@ -567,7 +579,7 @@
 
     n2_z = link(n2_all.at[z, x], n2_all.at[z, x], peer(dz=1))
     n2_x = link(n2_all.at[z, x], n2_all.at[z, x], peer(dx=1))
-    n2_zx_sem = take()
+    n2_far = take(2)
     g_x.wait_recv()
     g_zx.wait_recv()
 
@@ -588,7 +600,10 @@
         copy.wait_recv()
 
     po_base = take(3)
-    pg_base = take(3)
+    pg_base = take(6)
+
+    def wait_block(block_ref, sem):
+        pltpu.make_async_copy(block_ref, block_ref, sem).wait()
 
     @pl.loop(0, 4)
     def _(i):
@@ -601,11 +616,13 @@
         def _():
             n2_x.wait_recv()
             n2_z.wait_recv()
-            link(n2_all.at[flip(z, 1), x], n2_all.at[flip(z, 1), x], peer(dx=1), sem=n2_zx_sem)
+            link(n2_all.at[z, flip(x, 1), 0], n2_all.at[z, flip(x, 1), 0], peer(dz=1), sem=n2_far)
+            link(n2_all.at[flip(z, 1), x, 1], n2_all.at[flip(z, 1), x, 1], peer(dx=1), sem=n2_far + 1)
 
         @pl.when(i == 3)
         def _():
-            pltpu.make_async_copy(chunk, chunk, rsem.at[n2_zx_sem]).wait()
+            wait_block(chunk.at[0], rsem.at[n2_far])
+            wait_block(chunk.at[1], rsem.at[n2_far + 1])
 
         @pl.loop(0, tiles)
         def _(t):
@@ -634,7 +651,11 @@
 
         @pl.when(dx == 1)
         def _():
-            link(pg_s.at[cz, cx], pg_r.at[dz], peer(dx=1), sem=pg_base + dz)
+            link(pg_s.at[cz, cx, 0], pg_r.at[dz, 0], peer(dx=1), sem=pg_base + 2 * dz)
+
+        @pl.when(dz == 1)
+        def _():
+            link(pg_s.at[cz, cx, 1], pg_r.at[dx, 1], peer(dz=1), sem=pg_base + 2 * dx + 1)
 
         @pl.loop(0, tiles)
         def _(t):
@@ -651,7 +672,8 @@
         copy.wait_send()
     for copy in (n2_z, n2_x, g_z, g_x, g_zx):
         copy.wait_send()
-    pltpu.make_async_copy(n2_all.at[z, x], n2_all.at[z, x], ssem.at[n2_zx_sem]).wait()
+    wait_block(n2_all.at[z, x, 0], ssem.at[n2_far])
+    wait_block(n2_all.at[z, x, 1], ssem.at[n2_far + 1])
     for flips in order:
         ref = wgu_all.at[slab(*flips)]
         pltpu.make_async_copy(ref, ref, ssem.at[gu_sems[flips]]).wait()
@@ -671,21 +693,17 @@
 
     gu_swap = link(gu_grad.at[:, :, :, flip(c, 1)], gu_core, peer(dc=1))
 
-    def wait_block(block_ref, sem):
-        pltpu.make_async_copy(block_ref, block_ref, sem).wait()
-
-    def partial_z(sent, came, base):
-        wait_block(came.at[1], rsem.at[base + 1])
-
-        @pl.loop(0, 4)
+    def add_blocks(ref, came):
+        @pl.loop(0, 2)
         def _(m):
-            at = (m // 2, m % 2)
-            ref = sent.at[(flip(z, 1), x) + at]
-            ref[...] = (ref[...].astype(f32) + came[(1,) + at].astype(f32)).astype(bf16)
-
-        return link(sent.at[flip(z, 1), x], came.at[2], peer(dz=1), sem=base + 2)
-
-    partial_z(pg_s, pg_r, pg_base)
+            ref[m] = (ref[m].astype(f32) + came[m].astype(f32)).astype(bf16)
+
+    wait_block(pg_r.at[1, 0], rsem.at[pg_base + 2])
+    wait_block(pg_r.at[1, 1], rsem.at[pg_base + 3])
+    add_blocks(pg_s.at[flip(z, 1), x, 0], pg_r.at[1, 0])
+    link(pg_s.at[flip(z, 1), x, 0], pg_r.at[2, 0], peer(dz=1), sem=pg_base + 4)
+    add_blocks(pg_s.at[z, flip(x, 1), 1], pg_r.at[1, 1])
+    link(pg_s.at[z, flip(x, 1), 1], pg_r.at[2, 1], peer(dx=1), sem=pg_base + 5)
 
     down_grad = wd_all
 
@@ -710,10 +728,23 @@
         ref = gu_grad.at[at + (c,)]
         ref[...] = (ref[...].astype(f32) + gu_core[at].astype(f32)).astype(bf16)
 
+    def gu_parts(flips):
+        j = z * 2 + x
+        for u in range(2):
+            for part in range(2):
+                src = gu_grad.at[slab(*flips) + (slice(None), pl.ds(u * block + part * half, half))]
+                cols = pl.ds(pl.multiple_of(u * ff + part * (ff // 2) + j * half, half), half)
+                yield src, gu_out.at[flips[0], :, cols]
+
     gu_sends = []
     for flips in order:
-        gu_sends.append(link(gu_grad.at[slab(*flips)], gu_out.at[s, z, x], peer(*flips)))
-    gu_keep = local(gu_grad.at[slab()], gu_out.at[s, z, x])
+        gu_sends.append(take())
+        for src, dst in gu_parts(flips):
+            link(src, dst, peer(*flips), sem=gu_sends[-1])
+    gu_keep = lsem.at[lcount[0]]
+    lcount[0] += 1
+    for src, dst in gu_parts((0, 0, 0)):
+        pltpu.make_async_copy(src, dst, gu_keep).start()
 
     down_swap.wait_recv()
 
@@ -727,10 +758,13 @@
     down_send = link(down_grad.at[flip(s, 1), c], down_out.at[1], peer(ds=1))
     down_keep = local(down_grad.at[s, c], down_out.at[0])
 
-    partial_z(po_s, po_r, po_base)
-
-    for i in (0, 2):
-        wait_block(pg_r.at[i], rsem.at[pg_base + i])
+    wait_block(po_r.at[1], rsem.at[po_base + 1])
+    add_blocks(po_s.at[flip(z, 1), x, 0], po_r.at[1, 0])
+    add_blocks(po_s.at[flip(z, 1), x, 1], po_r.at[1, 1])
+    link(po_s.at[flip(z, 1), x], po_r.at[2], peer(dz=1), sem=po_base + 2)
+
+    for i in (0, 1, 4, 5):
+        wait_block(pg_r.at[i // 2, i % 2], rsem.at[pg_base + i])
     gsum_s[...] = jnp.zeros_like(gsum_s)
 
     def add_gain(which, value):
@@ -749,7 +783,7 @@
         add_gain(1, jnp.sum(g_n2 * hidden * inv, axis=0, keepdims=True))
         scaled = g_n2 * gain_row(1)
         inner = jnp.mean(scaled * hidden, axis=-1, keepdims=True)
-        g_sum = cot_ref[part].astype(f32) * mask_ref[part]
+        g_sum = cot_ref[part].astype(f32) * mask[part][:, :1]
         g_mid = g_sum + inv * scaled - hidden * (inv * inv * inv * inner)
         gmid[part] = g_mid
         gattn[part] = g_mid.astype(bf16)
@@ -760,7 +794,7 @@
             cols = pl.ds(pl.multiple_of(t * tile, tile), tile)
             dest[:, cols] = dot_nt(left[...], wa[g, t // 2, t % 2].reshape(tile, width))
 
-    g_mixed = ig_ref
+    g_mixed = gwide
     project_back(gattn, OUT, g_mixed)
 
     @pl.loop(0, steps)
@@ -835,8 +869,9 @@
     def leg_cross(g):
         legs[g][2].wait_recv()
         add_into(g, 2, lambda m: (m, z, x, c), lambda m: attn_z.at[g, m])
-        legs[g].append(link(grad_view(g, flip(s, 1), z, x, c), attn_out.at[1, g], peer(ds=1)))
-        legs[g].append(local(grad_view(g, s, z, x, c), attn_out.at[0, g]))
+        cols = pl.ds({QUERY: 0, KEY: 1, VALUE: 2, OUT: 3}[g] * width, width)
+        legs[g].append(link(grad_view(g, flip(s, 1), z, x, c), attn_out.at[1, :, cols], peer(ds=1)))
+        legs[g].append(local(grad_view(g, s, z, x, c), attn_out.at[0, :, cols]))
 
     weight_grad(OUT, mixed, gattn)
     weight_grad(QUERY, normed, gq)
@@ -869,7 +904,7 @@
     def _(t):
         cols = pl.ds(pl.multiple_of(t * tile, tile), tile)
         at = (t // 2, t % 2)
-        ig_ref[:, cols] = (
+        gwide[:, cols] = (
             dot_nt(gq[...], wa[(QUERY,) + at].reshape(tile, width))
             + dot_nt(gk[...], wa[(KEY,) + at].reshape(tile, width))
             + dot_nt(gv[...], wa[(VALUE,) + at].reshape(tile, width))
@@ -880,11 +915,14 @@
         part = pl.ds(i * rows, rows)
         hidden = x_ref[part].astype(f32)
         inv = r_one[part][:, :1]
-        g_n1 = ig_ref[part]
+        g_n1 = gwide[part]
         add_gain(0, jnp.sum(g_n1 * hidden * inv, axis=0, keepdims=True))
         scaled = g_n1 * gain_row(0)
         inner = jnp.mean(scaled * hidden, axis=-1, keepdims=True)
-        ig_ref[part] = gmid[part] + inv * scaled - hidden * (inv * inv * inv * inner)
+        grad = gmid[part] + inv * scaled - hidden * (inv * inv * inv * inner)
+        for k in range(width // 128):
+            spread = pl.ds(i * rows * (width // 128) + k, rows, width // 128)
+            ig_ref[spread, :] = grad[:, k * 128 : (k + 1) * 128]
 
     def gain_sum_copy(r):
         to = lax.rem(f + r, 16)
@@ -913,24 +951,33 @@
         total = po_s[(z, x) + at].astype(f32)
         for k in (0, 2):
             total += po_r[(k,) + at].astype(f32)
-        out_ref[part] = (mask_ref[part] * (hmid[part] + total)).astype(bf16)
+        out_ref[part] = (mask[part][:, :1] * (hmid[part] + total)).astype(bf16)
 
     leg_cross(KEY)
-    gain_out[...] = gsum_s[f // per_block]
+    gsum_r[15] = gsum_s[f // per_block]
 
     @pl.loop(1, 16)
     def _(r):
         gain_sum_copy(r).wait()
-        gain_out[...] += gsum_r[r - 1]
+        gsum_r[15] += gsum_r[r - 1]
+
+    gain_sum = jnp.where(f % per_block == 0, 1.0, 0.0) * gsum_r[15][:, :rows]
+    for b in range(1, per_block):
+        gain_sum += jnp.where(f % per_block == b, 1.0, 0.0) * gsum_r[15][:, b * rows : (b + 1) * rows]
+    gain_one_out[...] = gain_sum[0:1]
+    gain_two_out[...] = gain_sum[1:2]
 
     for copy in keep + [k_copy, v_copy, gv_copy, gk_copy, gu_swap, down_swap]:
         copy.wait_send()
     for i in range(3):
         wait_block(po_r.at[i], ssem.at[po_base + i])
-        wait_block(pg_r.at[i], ssem.at[pg_base + i])
-    for copy in gu_sends + [down_send]:
-        copy.wait()
-    gu_keep.wait()
+        wait_block(pg_r.at[i, 0], ssem.at[pg_base + 2 * i])
+        wait_block(pg_r.at[i, 1], ssem.at[pg_base + 2 * i + 1])
+    down_send.wait()
+    wait_block(gu_grad.at[slab()], gu_keep)
+    for sem in gu_sends:
+        wait_block(gu_grad.at[slab()], ssem.at[sem])
+        wait_block(gu_grad.at[slab()], rsem.at[sem])
     down_keep.wait()
     for g in (OUT, QUERY, VALUE, KEY):
         for copy in legs[g][:3]:
@@ -945,13 +992,7 @@
     block = width
     f32, bf16 = jnp.float32, jnp.bfloat16
     lane_block = 128
-    per_block = lane_block // rows
-    f = lax.axis_index("fsdp")
     lane_blocks = width // lane_block
-    gains = jnp.concatenate([attn_gain[0], ffn_gain[0]], axis=0)
-    gains = jnp.concatenate([jnp.where(f % per_block == b, gains, 0) for b in range(per_block)], axis=1).astype(bf16)
-    gains = jnp.pad(gains, ((0, 14), (0, 0)))
-    mask = frame_flags.astype(f32)[:, None]
     vmem = pl.BlockSpec(memory_space=pltpu.VMEM)
     anywhere = pl.BlockSpec(memory_space=pl.ANY)
     unit = (2, 2, 2, 2, rows, width)
@@ -992,6 +1033,9 @@
         pltpu.VMEM(own, f32),
         pltpu.VMEM(own, bf16),
         pltpu.VMEM(own, f32),
+        pltpu.VMEM(own, f32),
+        pltpu.VMEM((tokens, 128), f32),
+        pltpu.VMEM((16, lane_block), bf16),
         pltpu.VMEM((tokens, 128), f32),
         pltpu.VMEM((tokens, 128), f32),
         pltpu.VMEM((tokens, 128), f32),
@@ -999,7 +1043,7 @@
         pltpu.VMEM((15, 16, lane_block), bf16),
         pltpu.VMEM((lane_blocks, 16, lane_block), f32),
         pltpu.VMEM((lane_blocks, 8, lane_block), f32),
-        pltpu.VMEM((15, 8, lane_block), f32),
+        pltpu.VMEM((16, 8, lane_block), f32),
         pltpu.VMEM((width, 128), bf16),
         pltpu.VMEM((128, width), bf16),
         pltpu.SemaphoreType.DMA((SEMS,)),
@@ -1014,41 +1058,38 @@
         square_kernel,
         out_shape=(
             jax.ShapeDtypeStruct(own, bf16),
-            jax.ShapeDtypeStruct(own, f32),
-            jax.ShapeDtypeStruct((8, lane_block), f32),
-            jax.ShapeDtypeStruct((2, 2, 2, rows, 2 * block), bf16),
+            jax.ShapeDtypeStruct((tokens * lane_blocks, lane_block), f32),
+            jax.ShapeDtypeStruct((1, rows), f32),
+            jax.ShapeDtypeStruct((1, rows), f32),
+            jax.ShapeDtypeStruct((2, rows, 8 * block), bf16),
             jax.ShapeDtypeStruct((2, 2, 2, rows, width), bf16),
-            jax.ShapeDtypeStruct((2, 4, rows, width), bf16),
+            jax.ShapeDtypeStruct((2, rows, 4 * width), bf16),
         ),
-        in_specs=[vmem] * 4 + [anywhere] * 4,
-        out_specs=(vmem, vmem, vmem, anywhere, anywhere, anywhere),
+        in_specs=[vmem] * 5 + [anywhere] * 4,
+        out_specs=(vmem, vmem, vmem, vmem, anywhere, anywhere, anywhere),
         scratch_shapes=scratch,
         compiler_params=pltpu.CompilerParams(
             collective_id=0, has_side_effects=True, vmem_limit_bytes=VMEM_BYTES
         ),
         cost_estimate=pl.CostEstimate(flops=26 * 10**9, bytes_accessed=2**23, transcendentals=2**21),
     )(
-        inputs[:, 0], cotangent[:, 0], mask, gains,
+        inputs[:, 0], cotangent[:, 0], frame_flags.reshape(tokens // lane_block, lane_block), attn_gain[0], ffn_gain[0],
         qkv_weight[0, 0], out_weight[0, 0], gate_up_weight[0, 0], down_weight[0, 0].reshape(2, 2, rows, width),
     )
-    result, input_grad, gain_sums, gu, down, attn = outs
-    gain_sums = sum(
-        jnp.where(f % per_block == b, gain_sums[:2, b * rows : (b + 1) * rows], 0.0) for b in range(per_block)
-    )
-    gu = gu.astype(f32)
-    gu = (gu[0] + gu[1]).reshape(4, rows, 2, 2, block // 2).transpose(1, 2, 3, 0, 4).reshape(1, 1, rows, 8 * block)
-    down = (down[0].astype(f32) + down[1].astype(f32)).reshape(down_weight.shape)
-    attn = attn[0].astype(f32) + attn[1].astype(f32)
-    qkv = jnp.concatenate([attn[QUERY], attn[KEY], attn[VALUE]], axis=1)[None, None]
+    result, input_grad, gain_one, gain_two, gu, down, attn = outs
+
+    def both(pair):
+        return pair[0].astype(f32) + pair[1].astype(f32)
+
     return (
         result[:, None],
-        input_grad[:, None],
-        gain_sums[0:1, None],
-        qkv,
-        attn[OUT][None, None],
-        gain_sums[1:2, None],
-        gu,
-        down,
+        input_grad.reshape(tokens, 1, width),
+        gain_one[None],
+        both(attn[:, :, : 3 * width])[None, None],
+        both(attn[:, :, 3 * width :])[None, None],
+        gain_two[None],
+        both(gu)[None, None],
+        both(down).reshape(down_weight.shape),
     )
 
 

time: 303 us -> 268 us (0.88)
  Pallas kernels: 282 us -> 258 us
  local copies, waits for them, and re-layouts: 14.4 us -> 2.81 us
    pallas_call x1, Pallas kernels: 282 us -> 258 us  [square_layer(): pl.pallas_call(square_kernel, out_shape=(jax.ShapeDtypeStruct(own, bf16),...]
    add x4, other arithmetic: 2.43 us -> 6.6 us  [both(): return pair[0].astype(f32) + pair[1].astype(f32)]
where the time goes in v3:
time: 268 us
  Pallas kernels  258 us (96%)
  other arithmetic  6.6 us (2%)
  local copies, waits for them, and re-layouts  2.81 us (1%)
    pallas_call x1, Pallas kernels, square_layer(): pl.pallas_call(square_kernel, out_shape=(jax.ShapeDtypeStruct(own, bf16),...  258 us
    add x4, other arithmetic, both(): return pair[0].astype(f32) + pair[1].astype(f32)  6.6 us

profile of v3, /device:TPU:0, one launch (start us, length us, event | category | flops | bytes accessed | tf_op | source)
XLA Modules:
  0.0 268.0 jit_solution(3662043668549022735)
XLA Ops:
  0.6 257.9 %shard_map.152 = (bf16[256,1024]{1,0:T(8,128)(2,1)}, f32[2048,128]{1,0:T(8,128)}, f32[1,64]{1,0:T(1,128)}, f32[1,64]{1,0:T(1,128)}, bf16[2,64,8192]{2,1,0:T(8,12...) custom-call(bf16[256,1024]{1,0:T(8,128)(2,1)} %bitcast.24, bf16[256,1024]{1,0:T(8,128)(2,1)} %bitcast.25, ...), custom_call_target="tpu_custom_call" | custom-call | flops 25999998976 | bytes 8388608 | tf_op jit(solution)/shard_map/pallas_call | solution.py:1057
  258.6 0.0 copy-start.2
  258.6 0.0 copy-start
  258.6 1.9 add_bitcast_fusion.2
  260.4 2.1 add_bitcast_fusion.1
  262.5 0.0 copy-done.2
  262.5 1.1 convert_add_fusion
  263.7 0.0 copy-done
  263.7 0.0 copy-start.3
  263.7 0.0 copy-start.1
  263.7 1.5 add_bitcast_fusion
  265.2 0.0 copy-done.3
  265.2 0.0 copy-start.5
  265.2 0.0 copy-start.4
  265.2 0.8 copy.22
  266.0 0.0 copy-done.1
  266.0 1.0 copy.23
  267.0 0.0 copy-done.5
  267.0 0.5 copy.24
  267.5 0.0 copy-done.4
  267.5 0.5 copy.25
Async XLA Ops:
  258.6 3.9 %copy-start.2 = (bf16[2,2,2,64,1024]{4,3,2,1,0:T(8,128)(2,1)S(1)}, bf16[2,2,2,64,1024]{4,3,2,1,0:T(8,128)(2,1)}, u32[]{:S(2)}) copy-start(bf16[2,2,2,64,1024]{4,3,2,1,0:T(8,128)(2,1)} %get-tuple-element.21) | copy-start | bytes 3145732
  258.6 5.1 %copy-start = (bf16[2,64,8192]{2,1,0:T(8,128)(2,1)S(1)}, bf16[2,64,8192]{2,1,0:T(8,128)(2,1)}, u32[]{:S(2)}) copy-start(bf16[2,64,8192]{2,1,0:T(8,128)(2,1)} %get-tuple-element.20) | copy-start | bytes 6291460
  263.7 1.5 copy-start.3
  263.7 2.3 copy-start.1
  265.2 1.8 copy-start.5
  265.2 2.3 copy-start.4

commit v4 on v0

--- a/solution.py
+++ b/solution.py
@@ -1,8 +1,11 @@
+import functools
 import math
 
 import jax
 import jax.numpy as jnp
 from jax import lax
+from jax.experimental import pallas as pl
+from jax.experimental.pallas import tpu as pltpu
 from jax.sharding import PartitionSpec as P
 
 D = 1024
@@ -253,6 +256,1018 @@
     return fetched
 
 
+KEY, VALUE, QUERY, OUT = 0, 1, 2, 3
+GROUPS = {"k": KEY, "v": VALUE, "q": QUERY, "o": OUT}
+SEND_SEMS, RECV_SEMS = 76, 92
+ROUTES = {"p0": "z", "p1": "z", "u0": "x", "u1": "x"}
+MESH = pl.DeviceIdType.MESH
+
+
+class Names:
+    def __getattr__(self, name):
+        return name
+
+
+step = Names()
+
+ORDER = (
+    step.v_to_z, step.k_to_s, step.v_to_x, step.v_to_s, step.k_to_z, step.v_from_z, step.q_to_s, step.k_from_s,
+    step.o_to_s, step.g_own, step.q_to_z, step.v_to_c, step.norm, step.k_to_c, step.v_from_s, step.q_to_x,
+    step.ends, step.o_to_z, step.o_from_s, step.o_to_x, step.k_from_sz, step.q_from_z, step.gz, step.v_from_sz,
+    step.gs, step.k_from_z, step.mask, step.q_from_s, step.k_to_x, step.gd, step.o_to_c, step.v_from_x,
+    step.v_from_c, step.gx, step.d_to, step.cz, step.v_rows, step.gs_from, step.q_from_sz, step.cx, step.k_from_x,
+    step.q_to_c, step.o_from_sz, step.gx_from, step.q_from_x, step.gd_from, step.q_from_c, step.k_from_c,
+    step.gz_from, step.k_rows, step.g_own_from, step.o_from_z, step.czx, step.q_rows, step.attn, step.o_from_x,
+    step.o_from_c, step.mid, step.nz, step.d_from, step.gxs_from, step.nx, step.gzs_from, step.gds_from, step.ffn,
+    step.nzx, step.f2, step.p0n, step.f1, step.b1, step.u1n, step.p1n, step.f0, step.u0n, step.f3, step.p1f,
+    step.b3, step.w11, step.p0f, step.u0f, step.b2, step.y11, step.b0, step.p1t, step.u0t, step.w01, step.p0t,
+    step.dg, step.u1f, step.dy, step.gmid, step.gmix, step.Wo, step.w10, step.gk, step.Xo, step.w00, step.y01,
+    step.Wq, step.Xq, step.u1t, step.Wv, step.Zo, step.Xv, step.y10, step.Wk, step.Xk, step.Zq, step.out, step.Zv,
+    step.Sq, step.ig, step.Zk, step.So, step.Sv, step.y00, step.Sk, step.gain,
+)
+
+
+def flip(bit, change):
+    return bit + change - 2 * bit * change
+
+
+def square_kernel(
+    x_in, cot_in, flags_ref, gain_one_ref, gain_two_ref, wqkv, wout, wgu, wd,
+    out_hbm, ig_hbm, gain_one_out, gain_two_out, gu_out, down_out, attn_out,
+    wa, wgu_all, wd_all, n2_all, g_all, act_all, ggu_all,
+    po_s, po_r, pg_s, pg_r, gu_core, gu_cross, down_core, attn_core, attn_x, attn_z,
+    normed, qb, kb, vb, krem, vrem, mixed, hmid, gv_s, gk_s, gv_r, gk_r,
+    gq, gk, gv, gmid, gattn, hold_k, gwide, mask, gain_ref, p_own, p_rem, r_one, r_two,
+    gain_r, gain_f, gsum_s, gsum_r, ends, ends_t,
+    x_ref, cot_ref, out_ref, ig_ref, ssem, rsem, lsem, gsem,
+):
+    tokens, width = x_ref.shape
+    rows = width // 16
+    block = 4 * width // 4
+    half = block // 2
+    ff = 4 * width
+    f = lax.axis_index("fsdp")
+    y = lax.axis_index("pos")
+    c = f % 2
+    x = (f // 2) % 2
+    z = (f // 4) % 2
+    s = f // 8
+    f32, bf16 = jnp.float32, jnp.bfloat16
+    every = slice(None)
+    steps = tokens // rows
+    tile = 256
+    tiles = width // tile
+    scale = 1.0 / math.sqrt(HEAD_DIM)
+    lane_block = 128
+    per_block = lane_block // rows
+
+    def peer(ds=0, dz=0, dx=0, dc=0):
+        return flip(s, ds) * 8 + flip(z, dz) * 4 + flip(x, dx) * 2 + flip(c, dc)
+
+    def slab(ds=0, dz=0, dx=0, dc=0):
+        return flip(s, ds), flip(z, dz), flip(x, dx), flip(c, dc)
+
+    counter = [0, 0, 0]
+    sent = {}
+    coming = {}
+    actions = {}
+
+    def action(name):
+        def keep(fn):
+            actions[name] = fn
+
+        return keep
+
+    groups = {}
+
+    def take(which, group=None):
+        if group is not None and (which, group) in groups:
+            return groups[which, group]
+        counter[which] += 1
+        assert counter[which] <= (SEND_SEMS, RECV_SEMS)[which]
+        groups[which, group] = counter[which] - 1
+        return counter[which] - 1
+
+    def link(name, src, dst, to, to_y=None, send_group=None, recv_group=None):
+        copy = pltpu.make_async_remote_copy(
+            src_ref=src, dst_ref=dst, send_sem=ssem.at[take(0, send_group)], recv_sem=rsem.at[take(1, recv_group)],
+            device_id=(to, y if to_y is None else to_y), device_id_type=MESH,
+        )
+        copy.start()
+        if send_group is None:
+            sent[name] = copy
+        else:
+            coming[name] = copy
+
+    def local(name, src, dst):
+        counter[2] += 1
+        copy = pltpu.make_async_copy(src, dst, lsem.at[counter[2] - 1])
+        copy.start()
+        sent[name] = copy
+
+    def wait_block(ref, sem):
+        pltpu.make_async_copy(ref, ref, sem).wait()
+
+    freed = set()
+
+    def free(*names):
+        for name in names:
+            if name not in freed:
+                freed.add(name)
+                sent[name].wait_send()
+
+    def dot(a, b):
+        return jnp.dot(a, b, preferred_element_type=f32)
+
+    def dot_nt(a, b):
+        return lax.dot_general(a, b, (((1,), (1,)), ((), ())), preferred_element_type=f32)
+
+    def split(v):
+        high = v.astype(bf16)
+        return high, (v - high.astype(f32)).astype(bf16)
+
+    def head_sum(v):
+        high, low = split(v)
+        return dot(high, ends[...]) + dot(low, ends[...])
+
+    def head_spread(p):
+        high, low = split(p)
+        return dot(high, ends_t[...]) + dot(low, ends_t[...])
+
+    def add_rows(ref, came):
+        ref[...] = (ref[...].astype(f32) + came[...].astype(f32)).astype(bf16)
+
+    local("x_in", x_in, x_ref)
+    local("cot_in", cot_in, cot_ref)
+
+    barrier = pltpu.get_barrier_semaphore()
+
+    @pl.loop(1, 16)
+    def _(r):
+        pl.semaphore_signal(barrier, inc=1, device_id=(lax.rem(f + r, 16), y), device_id_type=MESH)
+
+    pl.semaphore_signal(barrier, inc=1, device_id=(f, 1 - y), device_id_type=MESH)
+
+    lanes = lax.broadcasted_iota(jnp.int32, gain_ref.shape, 1) // rows == f % per_block
+    sublane = lax.broadcasted_iota(jnp.int32, gain_ref.shape, 0)
+
+    def lane_tile(ref):
+        return jnp.concatenate([ref[...].astype(f32)] * per_block, axis=1)
+
+    gains = jnp.where(sublane == 0, lane_tile(gain_one_ref), jnp.where(sublane == 1, lane_tile(gain_two_ref), 0.0))
+    gain_ref[...] = jnp.where(lanes, gains, 0.0).astype(bf16)
+
+    pl.semaphore_wait(barrier, 16)
+
+    def gain_copy(r):
+        return pltpu.make_async_remote_copy(
+            src_ref=gain_ref, dst_ref=gain_r.at[r - 1], send_sem=gsem.at[0], recv_sem=gsem.at[1],
+            device_id=(lax.rem(f + r, 16), y), device_id_type=MESH,
+        )
+
+    def gain_row(which):
+        return jnp.concatenate([gain_f[i, which : which + 1, :] for i in range(gain_f.shape[0])], axis=1)
+
+    def add_gain(which, value):
+        for i in range(gsum_s.shape[0]):
+            gsum_s[i, which : which + 1, :] += value[:, i * 128 : (i + 1) * 128]
+
+    @pl.loop(1, 16)
+    def _(r):
+        gain_copy(r).start()
+
+    own_cols = (
+        wqkv.at[:, pl.ds(width, width)],
+        wqkv.at[:, pl.ds(2 * width, width)],
+        wqkv.at[:, pl.ds(0, width)],
+        wout,
+    )
+    ways = {"s": (1, 0, 0, 0), "z": (0, 1, 0, 0), "x": (0, 0, 1, 0), "c": (0, 0, 0, 1)}
+
+    def gather_actions(letter, g):
+        def send(name, way, src, dst):
+            recv_group = letter + "c" if way == "c" else None
+            link(letter + name, src, dst, peer(*ways[way]), send_group=letter + way, recv_group=recv_group)
+
+        def own(way):
+            @action(letter + "_to_" + way)
+            def _():
+                send(way, way, own_cols[g], wa.at[(g,) + slab()])
+                if way == "c":
+                    local(letter + "own", own_cols[g], wa.at[(g,) + slab()])
+
+        for way in ways:
+            own(way)
+
+        def pass_on(name, at, way):
+            ref = wa.at[(g,) + slab(*at)]
+            send(name, way, ref, ref)
+
+        @action(letter + "_from_s")
+        def _():
+            coming[letter + "s"].wait_recv()
+            pass_on("sz", (1, 0, 0, 0), "z")
+            pass_on("sx", (1, 0, 0, 0), "x")
+            pass_on("sc", (1, 0, 0, 0), "c")
+
+        @action(letter + "_from_z")
+        def _():
+            coming[letter + "z"].wait_recv()
+            pass_on("zx", (0, 1, 0, 0), "x")
+            pass_on("zc", (0, 1, 0, 0), "c")
+
+        @action(letter + "_from_sz")
+        def _():
+            coming[letter + "sz"].wait_recv()
+            pass_on("szx", (1, 1, 0, 0), "x")
+            pass_on("szc", (1, 1, 0, 0), "c")
+
+        @action(letter + "_from_x")
+        def _():
+            for name, at in (("x", (0, 0, 1, 0)), ("sx", (1, 0, 1, 0)), ("zx", (0, 1, 1, 0)), ("szx", (1, 1, 1, 0))):
+                coming[letter + name].wait_recv()
+                pass_on(name + "c", at, "c")
+
+        @action(letter + "_from_c")
+        def _():
+            sent[letter + "own"].wait()
+            wait_block(wa.at[g, :, :, :, flip(c, 1)], rsem.at[take(1, letter + "c")])
+
+    for letter, g in GROUPS.items():
+        gather_actions(letter, g)
+
+    @action("ends")
+    def _():
+        ends[...] = (
+            lax.broadcasted_iota(jnp.int32, ends.shape, 0) // HEAD_DIM
+            == lax.broadcasted_iota(jnp.int32, ends.shape, 1)
+        ).astype(bf16)
+        ends_t[...] = (
+            lax.broadcasted_iota(jnp.int32, ends_t.shape, 1) // HEAD_DIM
+            == lax.broadcasted_iota(jnp.int32, ends_t.shape, 0)
+        ).astype(bf16)
+
+    @action("mask")
+    def _():
+        sent["cot_in"].wait()
+        for i in range(tokens // 128):
+            flags = flags_ref[i : i + 1, :].astype(f32)
+            mask[i * 128 : (i + 1) * 128] = jnp.broadcast_to(flags, (128, 128)).T
+        g_all[z, x] = (cot_ref[...].astype(f32) * mask[:, :1]).astype(bf16).reshape(2, 2, rows, width)
+
+    @action("norm")
+    def _():
+        sent["x_in"].wait()
+        gain_f[...] = jnp.zeros_like(gain_f)
+        gain_f[f // per_block] += gain_ref[...].astype(f32)
+
+        wait_block(gain_r, gsem.at[0])
+        wait_block(gain_r, gsem.at[1])
+
+        @pl.loop(1, 16)
+        def _(r):
+            gain_f[lax.rem(f + 16 - r, 16) // per_block] += gain_r[r - 1].astype(f32)
+
+        @pl.loop(0, steps, unroll=True)
+        def _(i):
+            part = pl.ds(i * rows, rows)
+            hidden = x_ref[part].astype(f32)
+            inv = lax.rsqrt(jnp.mean(hidden * hidden, axis=-1, keepdims=True) + EPSILON)
+            r_one[part] = jnp.broadcast_to(inv, (rows, 128))
+            normed[part] = (hidden * inv * gain_row(0)).astype(bf16)
+
+    def project(left, g, dest):
+        @pl.loop(0, tiles, unroll=True)
+        def _(t):
+            cols = pl.ds(pl.multiple_of(t * tile, tile), tile)
+            dest[:, cols] = dot(left[...], wa[g, :, :, :, :, :, cols].reshape(width, tile)).astype(dest.dtype)
+
+    @action("k_rows")
+    def _():
+        project(normed, KEY, kb)
+        link("key", kb, krem, f, to_y=1 - y)
+
+    @action("v_rows")
+    def _():
+        project(normed, VALUE, vb)
+        link("value", vb, vrem, f, to_y=1 - y)
+
+    @action("q_rows")
+    def _():
+        project(normed, QUERY, qb)
+
+    blocks = {"s": (1, 0, 0), "x": (0, 0, 1), "z": (0, 1, 0), "d": (0, 1, 1)}
+    gu_sems = {}
+
+    def gu_in(flips):
+        j = flip(z, flips[1]) * 2 + flip(x, flips[2])
+        for u in range(2):
+            for part in range(2):
+                src = wgu.at[:, pl.ds(pl.multiple_of(u * ff + part * (ff // 2) + j * half, half), half)]
+                yield src, wgu_all.at[s, z, x, c, :, pl.ds(u * block + part * half, half)]
+
+    def pieces(flips, pairs):
+        sem = take(0), take(1)
+        for src, dst in pairs:
+            pltpu.make_async_remote_copy(
+                src_ref=src, dst_ref=dst, send_sem=ssem.at[sem[0]], recv_sem=rsem.at[sem[1]],
+                device_id=(peer(*flips), y), device_id_type=MESH,
+            ).start()
+        return sem
+
+    def pieces_local(pairs):
+        counter[2] += 1
+        sem = lsem.at[counter[2] - 1]
+        for src, dst in pairs:
+            pltpu.make_async_copy(src, dst, sem).start()
+        return sem
+
+    def gu_core_send(ref):
+        link("gc", ref, ref, peer(dc=1), send_group="g", recv_group="g")
+
+    def gu_actions(way, flips):
+        @action("g" + way)
+        def _():
+            gu_sems[flips] = pieces(flips, gu_in(flips))
+
+        @action("g" + way + "_from")
+        def _():
+            ref = wgu_all.at[slab(*flips)]
+            wait_block(ref, rsem.at[gu_sems[flips][1]])
+            if way != "s":
+                link("g" + way + "s", ref, ref, peer(ds=1))
+            gu_core_send(ref)
+
+        @action("g" + way + "s_from")
+        def _():
+            sent["g" + way + "s"].wait_recv()
+            ref = wgu_all.at[slab(1, flips[1], flips[2])]
+            gu_core_send(ref)
+
+    for way, flips in blocks.items():
+        gu_actions(way, flips)
+
+    @action("g_own")
+    def _():
+        gu_sems["own"] = pieces_local(gu_in((0, 0, 0)))
+
+    @action("g_own_from")
+    def _():
+        ref = wgu_all.at[slab()]
+        wait_block(ref, gu_sems["own"])
+        gu_core_send(ref)
+
+    @action("d_to")
+    def _():
+        own = wd_all.at[s, c]
+        link("ds", wd, own, peer(ds=1))
+        link("dc", wd, own, peer(dc=1))
+        local("down", wd, own)
+
+    @action("d_from")
+    def _():
+        sent["ds"].wait_recv()
+        ref = wd_all.at[flip(s, 1), c]
+        link("dsc", ref, ref, peer(dc=1))
+
+    @action("ffn")
+    def _():
+        wait_block(wgu_all.at[:, :, :, flip(c, 1)], rsem.at[take(1, "g")])
+        sent["down"].wait()
+        sent["dc"].wait_recv()
+        sent["dsc"].wait_recv()
+
+    @action("cx")
+    def _():
+        link("cx", g_all.at[z, x], g_all.at[z, x], peer(dx=1))
+
+    @action("cz")
+    def _():
+        link("cz", g_all.at[z, x], g_all.at[z, x], peer(dz=1))
+
+    @action("czx")
+    def _():
+        sent["cz"].wait_recv()
+        ref = g_all.at[flip(z, 1), x]
+        link("czx", ref, ref, peer(dx=1))
+
+    @action("attn")
+    def _():
+        sent["key"].wait_recv()
+        sent["value"].wait_recv()
+
+        @pl.loop(0, steps, unroll=True)
+        def _(i):
+            part = pl.ds(i * rows, rows)
+            query = qb[part].astype(f32)
+            own = head_sum(query * kb[part].astype(f32)) * scale
+            far = jnp.where(y > 0, head_sum(query * krem[part].astype(f32)) * scale, MASKED)
+            top = jnp.maximum(own, far)
+            own = jnp.exp(own - top)
+            far = jnp.exp(far - top)
+            total = own + far
+            own = own / total
+            far = far / total
+            p_own[part] = own
+            p_rem[part] = far
+            values = head_spread(own) * vb[part].astype(f32) + head_spread(far) * vrem[part].astype(f32)
+            mixed[part] = values.astype(bf16)
+
+    @action("mid")
+    def _():
+        project(mixed, OUT, hmid)
+
+        @pl.loop(0, steps, unroll=True)
+        def _(i):
+            part = pl.ds(i * rows, rows)
+            hidden = x_ref[part].astype(f32) + hmid[part]
+            hmid[part] = hidden
+            inv = lax.rsqrt(jnp.mean(hidden * hidden, axis=-1, keepdims=True) + EPSILON)
+            r_two[part] = jnp.broadcast_to(inv, (rows, 128))
+            n2_all[z, x, i // 2, i % 2] = (hidden * inv * gain_row(1)).astype(bf16)
+
+    @action("nx")
+    def _():
+        link("nx", n2_all.at[z, x], n2_all.at[z, x], peer(dx=1))
+
+    @action("nz")
+    def _():
+        link("nz", n2_all.at[z, x], n2_all.at[z, x], peer(dz=1))
+
+    @action("nzx")
+    def _():
+        sent["nz"].wait_recv()
+        ref = n2_all.at[flip(z, 1), x]
+        link("nzx", ref, ref, peer(dx=1))
+
+    def chunk_actions(i):
+        dz, dx = i // 2, i % 2
+        cz, cx = flip(z, dz), flip(x, dx)
+
+        @action("f%d" % i)
+        def _():
+            if i == 1:
+                sent["cx"].wait_recv()
+                sent["nx"].wait_recv()
+            if i == 3:
+                sent["czx"].wait_recv()
+                sent["nzx"].wait_recv()
+
+            @pl.loop(0, tiles, unroll=True)
+            def _(t):
+                first = pl.multiple_of(t * tile, tile)
+                cols = pl.ds(first, tile)
+                n2 = n2_all[cz, cx].reshape(tokens, width)
+                gate = dot(n2, wgu_all[:, :, :, :, :, cols].reshape(width, tile))
+                up = dot(n2, wgu_all[:, :, :, :, :, pl.ds(block + first, tile)].reshape(width, tile))
+                g_act = dot_nt(g_all[cz, cx].reshape(tokens, width), wd_all[t // 2, t % 2].reshape(tile, width))
+                sig = 1.0 / (1.0 + jnp.exp(-gate))
+                silu = gate * sig
+                shape = (2, 2, rows, tile)
+                act_all[cz, cx, :, :, :, cols] = (silu * up).astype(bf16).reshape(shape)
+                g_gate = g_act * up * sig * (1.0 + gate * (1.0 - sig))
+                ggu_all[cz, cx, :, :, :, cols] = g_gate.astype(bf16).reshape(shape)
+                ggu_all[cz, cx, :, :, :, pl.ds(block + first, tile)] = (g_act * silu).astype(bf16).reshape(shape)
+
+            @pl.loop(0, tiles, unroll=True)
+            def _(t):
+                cols = pl.ds(pl.multiple_of(t * tile, tile), tile)
+                g_n2 = dot_nt(
+                    ggu_all[cz, cx].reshape(tokens, 2 * block), wgu_all[t // 2, t % 2].reshape(tile, 2 * block)
+                )
+                pg_s[cz, cx, :, :, :, cols] = g_n2.astype(bf16).reshape(2, 2, rows, tile)
+
+        @action("b%d" % i)
+        def _():
+            @pl.loop(0, tiles, unroll=True)
+            def _(t):
+                cols = pl.ds(pl.multiple_of(t * tile, tile), tile)
+                part = dot(act_all[cz, cx].reshape(tokens, block), wd_all[:, :, :, :, :, cols].reshape(block, tile))
+                po_s[cz, cx, :, :, :, cols] = part.astype(bf16).reshape(2, 2, rows, tile)
+
+    for i in range(4):
+        chunk_actions(i)
+
+    def sum_actions(name, sums, came, h, way):
+        first = {"x": (0, 1), "z": (1, 0)}[way]
+        second = (first[1], first[0])
+        one, two = peer(0, *first), peer(0, *second)
+
+        def part(flips):
+            return sums.at[flip(z, flips[0]), flip(x, flips[1]), h]
+
+        @action(name + "n")
+        def _():
+            link(name + "n", part(first), came.at[0, h], one)
+
+        @action(name + "f")
+        def _():
+            link(name + "f", part((1, 1)), came.at[1, h], one)
+
+        @action(name + "t")
+        def _():
+            sent[name + "f"].wait_recv()
+
+            @pl.loop(0, 2, unroll=True)
+            def _(m):
+                add_rows(part(second).at[m], came.at[1, h, m])
+
+            link(name + "t", part(second), came.at[2, h], two)
+
+    for name, way in ROUTES.items():
+        sums, came = (pg_s, pg_r) if name[0] == "p" else (po_s, po_r)
+        sum_actions(name, sums, came, int(name[1]), way)
+
+    gu_grad = wgu_all
+    down_grad = wd_all
+
+    def gu_grad_out(flips):
+        j = z * 2 + x
+        for u in range(2):
+            for part in range(2):
+                src = gu_grad.at[slab(*flips) + (every, pl.ds(u * block + part * half, half))]
+                cols = pl.ds(pl.multiple_of(u * ff + part * (ff // 2) + j * half, half), half)
+                yield src, gu_out.at[:, cols]
+
+    def tile_actions(ds, dz):
+        tag = "%d%d" % (ds, dz)
+        at = flip(s, ds), flip(z, dz)
+
+        @action("w" + tag)
+        def _():
+            free("gxs", "gzs", "gds")
+            if "gc" not in freed:
+                freed.add("gc")
+                wait_block(wgu_all.at[:, :, :, c], ssem.at[take(0, "g")])
+            left = n2_all[:, :, :, :, :, pl.ds(pl.multiple_of((at[0] * 2 + at[1]) * tile, tile), tile)]
+            left = left.reshape(4 * tokens, tile).T
+
+            @pl.loop(0, block // tile, unroll=True)
+            def _(n):
+                wide = pl.ds(pl.multiple_of(n * 2 * tile, 2 * tile), 2 * tile)
+                part = dot(left, ggu_all[:, :, :, :, :, wide].reshape(4 * tokens, 2 * tile))
+                gu_grad[at[0], at[1], :, :, :, wide] = part.astype(bf16).reshape(2, 2, rows, 2 * tile)
+
+            link("w" + tag, gu_grad.at[at[0], at[1], :, flip(c, 1)], gu_core.at[at], peer(dc=1))
+
+        @action("y" + tag)
+        def _():
+            sent["w" + tag].wait_recv()
+            if ds == 0:
+                sent["y1%d" % dz].wait_recv()
+
+            @pl.loop(0, 2, unroll=True)
+            def _(m):
+                ref = gu_grad.at[at[0], at[1], m, c]
+                total = ref[...].astype(f32) + gu_core[at[0], at[1], m].astype(f32)
+                if ds == 0:
+                    total += gu_cross[at[1], m].astype(f32)
+                ref[...] = total.astype(bf16)
+
+            if ds == 1:
+                link("y" + tag, gu_grad.at[at[0], at[1], :, c], gu_cross.at[at[1]], peer(ds=1))
+                return
+            for dx in (1, 0):
+                flips = (0, dz, dx)
+                if flips == (0, 0, 0):
+                    gu_sems["keep"] = pieces_local(gu_grad_out(flips))
+                else:
+                    gu_sems[flips + (0,)] = pieces(flips, gu_grad_out(flips))
+
+    for ds in (0, 1):
+        for dz in (0, 1):
+            tile_actions(ds, dz)
+
+    @action("dg")
+    def _():
+        free("dsc")
+
+        @pl.loop(0, tiles, unroll=True)
+        def _(t):
+            cols = pl.ds(pl.multiple_of(t * tile, tile), tile)
+            left = act_all[:, :, :, :, :, cols].reshape(4 * tokens, tile).T
+
+            @pl.loop(0, width // (2 * tile), unroll=True)
+            def _(n):
+                wide = pl.ds(pl.multiple_of(n * 2 * tile, 2 * tile), 2 * tile)
+                part = dot(left, g_all[:, :, :, :, :, wide].reshape(4 * tokens, 2 * tile))
+                down_grad[t // 2, t % 2, :, :, :, wide] = part.astype(bf16).reshape(2, 2, rows, 2 * tile)
+
+        link("dg", down_grad.at[:, flip(c, 1)], down_core, peer(dc=1))
+
+    @action("dy")
+    def _():
+        sent["dg"].wait_recv()
+
+        @pl.loop(0, 8, unroll=2)
+        def _(m):
+            rest = ((m // 2) % 2, m % 2)
+            add_rows(down_grad.at[(m // 4, c) + rest], down_core.at[(m // 4,) + rest])
+
+        link("dy", down_grad.at[flip(s, 1), c], down_out.at[1], peer(ds=1))
+        local("dkeep", down_grad.at[s, c], down_out.at[0])
+
+    @action("gmid")
+    def _():
+        for name in ("p0n", "p1n", "p0t", "p1t"):
+            sent[name].wait_recv()
+        gsum_s[...] = jnp.zeros_like(gsum_s)
+
+        @pl.loop(0, steps, unroll=True)
+        def _(i):
+            part = pl.ds(i * rows, rows)
+            at = (i // 2, i % 2)
+            g_n2 = pg_s[(z, x) + at].astype(f32)
+            for k in (0, 2):
+                g_n2 += pg_r[(k,) + at].astype(f32)
+            hidden = hmid[part]
+            inv = r_two[part][:, :1]
+            add_gain(1, jnp.sum(g_n2 * hidden * inv, axis=0, keepdims=True))
+            scaled = g_n2 * gain_row(1)
+            inner = jnp.mean(scaled * hidden, axis=-1, keepdims=True)
+            g_sum = cot_ref[part].astype(f32) * mask[part][:, :1]
+            g_mid = g_sum + inv * scaled - hidden * (inv * inv * inv * inner)
+            gmid[part] = g_mid
+            gattn[part] = g_mid.astype(bf16)
+
+    @action("gmix")
+    def _():
+        @pl.loop(0, tiles, unroll=True)
+        def _(t):
+            cols = pl.ds(pl.multiple_of(t * tile, tile), tile)
+            gwide[:, cols] = dot_nt(gattn[...], wa[OUT, t // 2, t % 2].reshape(tile, width))
+
+        @pl.loop(0, steps, unroll=True)
+        def _(i):
+            part = pl.ds(i * rows, rows)
+            gv_s[part] = (head_spread(p_rem[part]) * gwide[part]).astype(bf16)
+
+        link("gv", gv_s, gv_r, f, to_y=1 - y)
+
+    @action("gk")
+    def _():
+        @pl.loop(0, steps, unroll=True)
+        def _(i):
+            part = pl.ds(i * rows, rows)
+            gm = gwide[part]
+            own, far = p_own[part], p_rem[part]
+            gp_own = head_sum(gm * vb[part].astype(f32))
+            gp_far = head_sum(gm * vrem[part].astype(f32))
+            inner = own * gp_own + far * gp_far
+            gs_own = head_spread(own * (gp_own - inner) * scale)
+            gs_far = head_spread(far * (gp_far - inner) * scale)
+            query = qb[part].astype(f32)
+            gk_s[part] = (gs_far * query).astype(bf16)
+            gq[part] = (gs_own * kb[part].astype(f32) + gs_far * krem[part].astype(f32)).astype(bf16)
+            hold_k[part] = gs_own * query
+
+        link("gk", gk_s, gk_r, f, to_y=1 - y)
+
+    stage = {OUT: act_all, QUERY: n2_all, VALUE: g_all, KEY: ggu_all}
+    out_cols = {QUERY: 0, KEY: 1, VALUE: 2, OUT: 3}
+
+    def grad_actions(letter, g):
+        def view(*at):
+            ref = stage[g]
+            if ref.shape[-1] != width:
+                return ref.at[at + (every,) * (5 - len(at)) + (pl.ds(0, width),)]
+            return ref.at[at]
+
+        def add_into(count, at_of, came):
+            @pl.loop(0, count, unroll=2)
+            def _(m):
+                add_rows(view(*at_of(m)), came(m))
+
+        def weight_grad(left, right):
+            @pl.loop(0, tiles, unroll=True)
+            def _(t):
+                cols = pl.ds(pl.multiple_of(t * tile, tile), tile)
+                part = dot(left[:, cols].T, right[...])
+                view(t // 2, t % 2)[...] = part.astype(bf16).reshape(2, 2, rows, width)
+
+            link("W" + letter, view(every, every, every, flip(c, 1)), attn_core.at[g], peer(dc=1))
+
+        @action("W" + letter)
+        def _():
+            if g == OUT:
+                weight_grad(mixed, gattn)
+            elif g == QUERY:
+                free("nx", "nz", "nzx")
+                weight_grad(normed, gq)
+            elif g == VALUE:
+                free("cx", "cz", "czx")
+                sent["gv"].wait_recv()
+
+                @pl.loop(0, steps, unroll=True)
+                def _(i):
+                    part = pl.ds(i * rows, rows)
+                    gv[part] = (head_spread(p_own[part]) * gwide[part] + gv_r[part].astype(f32)).astype(bf16)
+
+                weight_grad(normed, gv)
+            else:
+                sent["gk"].wait_recv()
+
+                @pl.loop(0, steps, unroll=True)
+                def _(i):
+                    part = pl.ds(i * rows, rows)
+                    gk[part] = (hold_k[part] + gk_r[part].astype(f32)).astype(bf16)
+
+                weight_grad(normed, gk)
+
+        @action("X" + letter)
+        def _():
+            sent["W" + letter].wait_recv()
+            add_into(
+                8,
+                lambda m: (m // 4, (m // 2) % 2, m % 2, c),
+                lambda m: attn_core.at[g, m // 4, (m // 2) % 2, m % 2],
+            )
+            link("X" + letter, view(every, every, flip(x, 1), c), attn_x.at[g], peer(dx=1))
+
+        @action("Z" + letter)
+        def _():
+            sent["X" + letter].wait_recv()
+            add_into(4, lambda m: (m // 2, m % 2, x, c), lambda m: attn_x.at[g, m // 2, m % 2])
+            link("Z" + letter, view(every, flip(z, 1), x, c), attn_z.at[g], peer(dz=1))
+
+        @action("S" + letter)
+        def _():
+            sent["Z" + letter].wait_recv()
+            add_into(2, lambda m: (m, z, x, c), lambda m: attn_z.at[g, m])
+            cols = pl.ds(out_cols[g] * width, width)
+            link("S" + letter, view(flip(s, 1), z, x, c), attn_out.at[1, :, cols], peer(ds=1))
+            local("keep" + letter, view(s, z, x, c), attn_out.at[0, :, cols])
+
+    for letter, g in GROUPS.items():
+        grad_actions(letter, g)
+
+    def gain_sum_copy(r):
+        to = lax.rem(f + r, 16)
+        return pltpu.make_async_remote_copy(
+            src_ref=gsum_s.at[to // per_block], dst_ref=gsum_r.at[r - 1],
+            send_sem=gsem.at[2], recv_sem=gsem.at[3],
+            device_id=(to, y), device_id_type=MESH,
+        )
+
+    @action("ig")
+    def _():
+        @pl.loop(0, tiles, unroll=True)
+        def _(t):
+            cols = pl.ds(pl.multiple_of(t * tile, tile), tile)
+            at = (t // 2, t % 2)
+            gwide[:, cols] = (
+                dot_nt(gq[...], wa[(QUERY,) + at].reshape(tile, width))
+                + dot_nt(gk[...], wa[(KEY,) + at].reshape(tile, width))
+                + dot_nt(gv[...], wa[(VALUE,) + at].reshape(tile, width))
+            )
+
+        @pl.loop(0, steps, unroll=True)
+        def _(i):
+            part = pl.ds(i * rows, rows)
+            hidden = x_ref[part].astype(f32)
+            inv = r_one[part][:, :1]
+            g_n1 = gwide[part]
+            add_gain(0, jnp.sum(g_n1 * hidden * inv, axis=0, keepdims=True))
+            scaled = g_n1 * gain_row(0)
+            inner = jnp.mean(scaled * hidden, axis=-1, keepdims=True)
+            grad = gmid[part] + inv * scaled - hidden * (inv * inv * inv * inner)
+            for k in range(width // 128):
+                spread = pl.ds(i * rows * (width // 128) + k, rows, width // 128)
+                ig_ref[spread, :] = grad[:, k * 128 : (k + 1) * 128]
+
+        local("keep_ig", ig_ref, ig_hbm)
+
+        @pl.loop(1, 16)
+        def _(r):
+            gain_sum_copy(r).start()
+
+    @action("gain")
+    def _():
+        gsum_r[15] = gsum_s[f // per_block]
+
+        wait_block(gsum_r.at[pl.ds(0, 15)], gsem.at[2])
+        wait_block(gsum_r.at[pl.ds(0, 15)], gsem.at[3])
+
+        @pl.loop(1, 16)
+        def _(r):
+            gsum_r[15] += gsum_r[r - 1]
+
+        gain_sum = jnp.where(f % per_block == 0, 1.0, 0.0) * gsum_r[15][:, :rows]
+        for b in range(1, per_block):
+            gain_sum += jnp.where(f % per_block == b, 1.0, 0.0) * gsum_r[15][:, b * rows : (b + 1) * rows]
+        gain_one_out[...] = gain_sum[0:1]
+        gain_two_out[...] = gain_sum[1:2]
+
+    @action("out")
+    def _():
+        for name in ("u0n", "u1n", "u0t", "u1t"):
+            sent[name].wait_recv()
+
+        @pl.loop(0, steps, unroll=True)
+        def _(i):
+            part = pl.ds(i * rows, rows)
+            at = (i // 2, i % 2)
+            total = po_s[(z, x) + at].astype(f32)
+            for k in (0, 2):
+                total += po_r[(k,) + at].astype(f32)
+            out_ref[part] = (mask[part][:, :1] * (hmid[part] + total)).astype(bf16)
+
+        local("keep_out", out_ref, out_hbm)
+
+    for name in ORDER:
+        actions[name]()
+
+    for letter in GROUPS:
+        sent["S" + letter].wait_recv()
+        sent["keep" + letter].wait()
+    sent["dy"].wait_recv()
+    sent["dkeep"].wait()
+    wait_block(gu_grad.at[slab()], gu_sems["keep"])
+    for flips in blocks.values():
+        wait_block(wgu_all.at[slab()], ssem.at[gu_sems[flips][0]])
+        if flips[0] == 0:
+            wait_block(gu_grad.at[slab()], ssem.at[gu_sems[flips + (0,)][0]])
+            wait_block(gu_grad.at[slab()], rsem.at[gu_sems[flips + (0,)][1]])
+    sent["keep_out"].wait()
+    sent["keep_ig"].wait()
+    for letter, g in GROUPS.items():
+        wait_block(wa.at[g, :, :, :, c], ssem.at[take(0, letter + "c")])
+        wait_block(wa.at[g, :, :, x, c], ssem.at[take(0, letter + "x")])
+        wait_block(wa.at[g, :, z, x, c], ssem.at[take(0, letter + "z")])
+        wait_block(wa.at[(g,) + slab()], ssem.at[take(0, letter + "s")])
+    free(*(name for name in sent if name not in ("down", "x_in", "cot_in") and not name.startswith(("keep", "dkeep"))
+           and not name.endswith("own")))
+
+
+def square_layer(inputs, frame_flags, attn_gain, qkv_weight, out_weight, ffn_gain, gate_up_weight, down_weight, cotangent):
+    tokens, _, width = inputs.shape
+    rows = qkv_weight.shape[2]
+    block = width
+    f32, bf16 = jnp.float32, jnp.bfloat16
+    lane_block = 128
+    lane_blocks = width // lane_block
+    vmem = pl.BlockSpec(memory_space=pltpu.VMEM)
+    anywhere = pl.BlockSpec(memory_space=pl.ANY)
+    unit = (2, 2, 2, 2, rows, width)
+    double = (2, 2, 2, 2, rows, 2 * block)
+    own = (tokens, width)
+    scratch = [
+        pltpu.VMEM((4,) + unit, bf16),
+        pltpu.VMEM(double, bf16),
+        pltpu.VMEM(unit, bf16),
+        pltpu.VMEM(unit, bf16),
+        pltpu.VMEM(unit, bf16),
+        pltpu.VMEM(unit, bf16),
+        pltpu.VMEM(double, bf16),
+        pltpu.VMEM(unit, bf16),
+        pltpu.VMEM((3, 2, 2, rows, width), bf16),
+        pltpu.VMEM(unit, bf16),
+        pltpu.VMEM((3, 2, 2, rows, width), bf16),
+        pltpu.VMEM((2, 2, 2, rows, 2 * block), bf16),
+        pltpu.VMEM((2, 2, rows, 2 * block), bf16),
+        pltpu.VMEM((2, 2, 2, rows, width), bf16),
+        pltpu.VMEM((4, 2, 2, 2, rows, width), bf16),
+        pltpu.VMEM((4, 2, 2, rows, width), bf16),
+        pltpu.VMEM((4, 2, rows, width), bf16),
+        pltpu.VMEM(own, bf16),
+        pltpu.VMEM(own, bf16),
+        pltpu.VMEM(own, bf16),
+        pltpu.VMEM(own, bf16),
+        pltpu.VMEM(own, bf16),
+        pltpu.VMEM(own, bf16),
+        pltpu.VMEM(own, bf16),
+        pltpu.VMEM(own, f32),
+        pltpu.VMEM(own, bf16),
+        pltpu.VMEM(own, bf16),
+        pltpu.VMEM(own, bf16),
+        pltpu.VMEM(own, bf16),
+        pltpu.VMEM(own, bf16),
+        pltpu.VMEM(own, bf16),
+        pltpu.VMEM(own, bf16),
+        pltpu.VMEM(own, f32),
+        pltpu.VMEM(own, bf16),
+        pltpu.VMEM(own, f32),
+        pltpu.VMEM(own, f32),
+        pltpu.VMEM((tokens, 128), f32),
+        pltpu.VMEM((16, lane_block), bf16),
+        pltpu.VMEM((tokens, 128), f32),
+        pltpu.VMEM((tokens, 128), f32),
+        pltpu.VMEM((tokens, 128), f32),
+        pltpu.VMEM((tokens, 128), f32),
+        pltpu.VMEM((15, 16, lane_block), bf16),
+        pltpu.VMEM((lane_blocks, 16, lane_block), f32),
+        pltpu.VMEM((lane_blocks, 8, lane_block), f32),
+        pltpu.VMEM((16, 8, lane_block), f32),
+        pltpu.VMEM((width, 128), bf16),
+        pltpu.VMEM((128, width), bf16),
+        pltpu.VMEM(own, bf16),
+        pltpu.VMEM(own, bf16),
+        pltpu.VMEM(own, bf16),
+        pltpu.VMEM((tokens * lane_blocks, lane_block), f32),
+        pltpu.SemaphoreType.DMA((SEND_SEMS,)),
+        pltpu.SemaphoreType.DMA((RECV_SEMS,)),
+        pltpu.SemaphoreType.DMA((16,)),
+        pltpu.SemaphoreType.DMA((4,)),
+    ]
+    outs = pl.pallas_call(
+        square_kernel,
+        out_shape=(
+            jax.ShapeDtypeStruct(own, bf16),
+            jax.ShapeDtypeStruct((tokens * lane_blocks, lane_block), f32),
+            jax.ShapeDtypeStruct((1, rows), f32),
+            jax.ShapeDtypeStruct((1, rows), f32),
+            jax.ShapeDtypeStruct((rows, 8 * block), bf16),
+            jax.ShapeDtypeStruct((2, 2, 2, rows, width), bf16),
+            jax.ShapeDtypeStruct((2, rows, 4 * width), bf16),
+        ),
+        in_specs=[anywhere] * 2 + [vmem] * 3 + [anywhere] * 4,
+        out_specs=(anywhere, anywhere, vmem, vmem, anywhere, anywhere, anywhere),
+        scratch_shapes=scratch,
+        compiler_params=pltpu.CompilerParams(
+            collective_id=0, has_side_effects=True, vmem_limit_bytes=VMEM_BYTES
+        ),
+        cost_estimate=pl.CostEstimate(flops=26 * 10**9, bytes_accessed=2**23, transcendentals=2**21),
+    )(
+        inputs[:, 0], cotangent[:, 0], frame_flags.reshape(tokens // lane_block, lane_block), attn_gain[0], ffn_gain[0],
+        qkv_weight[0, 0], out_weight[0, 0], gate_up_weight[0, 0], down_weight[0, 0].reshape(2, 2, rows, width),
+    )
+    result, input_grad, gain_one, gain_two, gu, down, attn = outs
+    grid = 2
+
+    def by_rows(shape):
+        return pl.BlockSpec((shape[0] // grid,) + shape[1:], lambda i: (i, 0))
+
+    def pair(shape):
+        return pl.BlockSpec((2, shape[0] // grid) + shape[1:], lambda i: (0, i, 0))
+
+    whole = pl.BlockSpec((1, rows), lambda i: (0, 0))
+    thin = (tokens * lane_blocks, lane_block)
+    result, input_grad, qkv, out, gu, down, gain_one, gain_two = pl.pallas_call(
+        finish_kernel,
+        grid=(grid,),
+        out_shape=(
+            jax.ShapeDtypeStruct(own, bf16),
+            jax.ShapeDtypeStruct(thin, f32),
+            jax.ShapeDtypeStruct((rows, 3 * width), f32),
+            jax.ShapeDtypeStruct((rows, width), f32),
+            jax.ShapeDtypeStruct((rows, 8 * block), f32),
+            jax.ShapeDtypeStruct(own, f32),
+            jax.ShapeDtypeStruct((1, rows), f32),
+            jax.ShapeDtypeStruct((1, rows), f32),
+        ),
+        in_specs=[by_rows(own), by_rows(thin), whole, whole, by_rows((rows, 8 * block)), pair(own), pair((rows, 4 * width))],
+        out_specs=[by_rows(own), by_rows(thin), by_rows((rows, 3 * width)), by_rows((rows, width)),
+                   by_rows((rows, 8 * block)), by_rows(own), whole, whole],
+        compiler_params=pltpu.CompilerParams(vmem_limit_bytes=VMEM_BYTES),
+    )(result, input_grad, gain_one, gain_two, gu, down.reshape((2,) + own), attn)
+    return (
+        result[:, None],
+        input_grad.reshape(tokens, 1, width),
+        gain_one[None],
+        qkv[None, None],
+        out[None, None],
+        gain_two[None],
+        gu[None, None],
+        down[None, None],
+    )
+
+
+def finish_kernel(
+    result, input_grad, gain_one, gain_two, gu, down, attn,
+    result_out, input_grad_out, qkv_out, out_out, gu_out, down_out, gain_one_out, gain_two_out,
+):
+    f32 = jnp.float32
+    width = out_out.shape[1]
+    result_out[...] = result[...]
+    input_grad_out[...] = input_grad[...]
+    gu_out[...] = gu[...].astype(f32)
+    down_out[...] = down[0].astype(f32) + down[1].astype(f32)
+    total = attn[0].astype(f32) + attn[1].astype(f32)
+    qkv_out[...] = total[:, : 3 * width]
+    out_out[...] = total[:, 3 * width :]
+    gain_one_out[...] = gain_one[...]
+    gain_two_out[...] = gain_two[...]
+
+
+VMEM_BYTES = 62 * 2**20
+
+
+def run_layer(axes, *args):
+    inputs, qkv_weight, down_weight = args[0], args[3], args[7]
+    tokens, places, width = inputs.shape
+    rows = qkv_weight.shape[2]
+    square = (
+        axes["fsdp"] == 16
+        and axes["pos"] == 2
+        and places == 1
+        and qkv_weight.shape[0] == 1
+        and tokens == 4 * rows
+        and down_weight.shape[2] == 4 * rows
+        and 128 % rows == 0
+    )
+    return square_layer(*args) if square else on_device(*args)
+
+
 def solution(mesh):
     in_specs = (
         P("fsdp", "pos", None),
@@ -276,5 +1291,5 @@
         P(None, "pos", "fsdp", None),
     )
     return jax.shard_map(
-        on_device, mesh=mesh, in_specs=in_specs, out_specs=out_specs, check_vma=False
-    )
+        functools.partial(run_layer, dict(mesh.shape)), mesh=mesh, in_specs=in_specs, out_specs=out_specs, check_vma=False
+    )

time: 1300 us -> 243 us (0.19); the launches traced: 1290 us -> 243 us
  waiting for transfers between devices: 1010 us -> 0 us
  Pallas kernels: 0 us -> 242 us
  matrix products: 143 us -> 0 us
  blocking collectives: 56.2 us -> 0 us
  local copies, waits for them, and re-layouts: 40.8 us -> 0 us
  between operations: 15.6 us -> 0.82 us
    reduce_scatter x4 -> x0, waiting for transfers between devices: 734 us -> none  [the longest x1 337 us: layer_backward(): lax.psum_scatter(gate_up_grad, 'fsdp', scatter_dimension=1, tiled=True)]
    pallas_call x0 -> x2, Pallas kernels: none -> 242 us  [the longest x1 238 us: square_layer(): pl.pallas_call(square_kernel, out_shape=(jax.ShapeDtypeStruct(own, bf16),...]
    all_gather x4 -> x0, waiting for transfers between devices: 186 us -> none  [the longest x1 95.4 us: ffn_weights(): lax.all_gather(gate_up_weight[layer_idx], 'fsdp', axis=1, tiled=True)]
    dot_general x18 -> x0, matrix products: 143 us -> none  [the longest x4 36.1 us: outer_sum(): jnp.einsum('fpd,fpe->pde', left_side, grad_rows, preferred_element_type=j...]
    all_to_all x3 -> x0, waiting for transfers between devices: 45.8 us -> none  [the longest x1 19.9 us: attention_forward(): lax.all_to_all(outgoing, 'pos', split_axis=0, concat_axis=2, tiled=True)[0]]
    unnamed x12 -> x0, waiting for transfers between devices: 41.2 us -> none
    unnamed x1 -> x0, blocking collectives: 35.2 us -> none
    all_to_all x1 -> x0, blocking collectives: 21.1 us -> none  [attention_backward(): lax.all_to_all(outgoing.astype(jnp.bfloat16), 'pos', split_axis=0, concat...]
  transfers between devices with their start and end apart: 13 -> 0, of which waited for: 11 -> 0; matrix products, arithmetic and copies ran while one was open for 9% -> 0% of each run, Pallas kernels for 0% -> 0%
where the time goes in v4:
time: 243 us
  Pallas kernels  242 us (100%)
    pallas_call x1, Pallas kernels, square_layer(): pl.pallas_call(square_kernel, out_shape=(jax.ShapeDtypeStruct(own, bf16),...  238 us

profile of v4, /device:TPU:0, one launch (start us, length us, event | category | flops | bytes accessed | tf_op | source)
XLA Modules:
  0.0 242.7 jit_solution(4927755299646803195)
XLA Ops:
  0.6 237.6 %shard_map.152 = (bf16[256,1024]{1,0:T(8,128)(2,1)}, f32[2048,128]{1,0:T(8,128)}, f32[1,64]{1,0:T(1,128)}, f32[1,64]{1,0:T(1,128)}, bf16[64,8192]{1,0:T(8,128)(2...) custom-call(bf16[256,1024]{1,0:T(8,128)(2,1)} %bitcast.24, bf16[256,1024]{1,0:T(8,128)(2,1)} %bitcast.25, ...), custom_call_target="tpu_custom_call" | custom-call | flops 25999998976 | bytes 8388608 | tf_op jit(solution)/shard_map/pallas_call | solution.py:1172
  238.3 4.3 %shard_map.153 = (bf16[256,1024]{1,0:T(8,128)(2,1)}, f32[2048,128]{1,0:T(8,128)}, f32[64,3072]{1,0:T(8,128)}, f32[64,1024]{1,0:T(8,128)}, f32[64,8192]{1,0:T(8,1...) custom-call(bf16[256,1024]{1,0:T(8,128)(2,1)} %get-tuple-element.23.result, ...), custom_call_target="tpu_custom_call" | custom-call | tf_op jit(solution)/shard_map/pallas_call | solution.py:1205

commit v5 on v4

--- a/solution.py
+++ b/solution.py
@@ -258,7 +258,7 @@
 
 KEY, VALUE, QUERY, OUT = 0, 1, 2, 3
 GROUPS = {"k": KEY, "v": VALUE, "q": QUERY, "o": OUT}
-SEND_SEMS, RECV_SEMS = 76, 92
+SEND_SEMS, RECV_SEMS = 51, 89
 ROUTES = {"p0": "z", "p1": "z", "u0": "x", "u1": "x"}
 MESH = pl.DeviceIdType.MESH
 
@@ -271,19 +271,19 @@
 step = Names()
 
 ORDER = (
-    step.v_to_z, step.k_to_s, step.v_to_x, step.v_to_s, step.k_to_z, step.v_from_z, step.q_to_s, step.k_from_s,
-    step.o_to_s, step.g_own, step.q_to_z, step.v_to_c, step.norm, step.k_to_c, step.v_from_s, step.q_to_x,
-    step.ends, step.o_to_z, step.o_from_s, step.o_to_x, step.k_from_sz, step.q_from_z, step.gz, step.v_from_sz,
-    step.gs, step.k_from_z, step.mask, step.q_from_s, step.k_to_x, step.gd, step.o_to_c, step.v_from_x,
-    step.v_from_c, step.gx, step.d_to, step.cz, step.v_rows, step.gs_from, step.q_from_sz, step.cx, step.k_from_x,
-    step.q_to_c, step.o_from_sz, step.gx_from, step.q_from_x, step.gd_from, step.q_from_c, step.k_from_c,
-    step.gz_from, step.k_rows, step.g_own_from, step.o_from_z, step.czx, step.q_rows, step.attn, step.o_from_x,
-    step.o_from_c, step.mid, step.nz, step.d_from, step.gxs_from, step.nx, step.gzs_from, step.gds_from, step.ffn,
-    step.nzx, step.f2, step.p0n, step.f1, step.b1, step.u1n, step.p1n, step.f0, step.u0n, step.f3, step.p1f,
-    step.b3, step.w11, step.p0f, step.u0f, step.b2, step.y11, step.b0, step.p1t, step.u0t, step.w01, step.p0t,
-    step.dg, step.u1f, step.dy, step.gmid, step.gmix, step.Wo, step.w10, step.gk, step.Xo, step.w00, step.y01,
-    step.Wq, step.Xq, step.u1t, step.Wv, step.Zo, step.Xv, step.y10, step.Wk, step.Xk, step.Zq, step.out, step.Zv,
-    step.Sq, step.ig, step.Zk, step.So, step.Sv, step.y00, step.Sk, step.gain,
+    step.v_to_c, step.k_to_x, step.mask, step.k_to_z, step.k_to_c, step.v_to_x, step.o_to_z, step.k_to_s,
+    step.v_to_s, step.q_to_s, step.o_to_c, step.gx, step.k_from_s, step.q_to_c, step.v_to_z, step.q_to_x,
+    step.o_to_s, step.k_from_sz, step.k_from_z, step.v_from_s, step.q_to_z, step.v_from_sz, step.o_from_s,
+    step.norm, step.gz, step.q_from_z, step.v_from_z, step.gs, step.q_from_s, step.v_from_x, step.v_from_c,
+    step.ends, step.gz_from, step.d_to, step.k_from_x, step.gd, step.v_rows, step.q_from_sz, step.cz, step.o_to_x,
+    step.cx, step.g_own, step.q_from_x, step.o_from_z, step.o_from_sz, step.g_own_from, step.q_from_c,
+    step.k_from_c, step.gx_from, step.k_rows, step.q_rows, step.gzs_from, step.attn, step.o_from_x, step.o_from_c,
+    step.mid, step.czx, step.gd_from, step.d_from, step.gs_from, step.nz, step.nx, step.gxs_from, step.gds_from,
+    step.nzx, step.ffn, step.f2, step.p1n, step.f1, step.b1, step.u1n, step.p0n, step.b2, step.f0, step.f3,
+    step.p1f, step.u0n, step.b3, step.w11, step.w01, step.p0f, step.u0f, step.y11, step.w10, step.p1t, step.b0,
+    step.w00, step.u0t, step.p0t, step.u1f, step.dg, step.dy, step.gmid, step.gmix, step.Wo, step.gk, step.u1t,
+    step.Xo, step.y01, step.Wq, step.y10, step.Wv, step.Xq, step.Xv, step.Zo, step.Wk, step.Xk, step.ig, step.Zq,
+    step.out, step.Zv, step.Sq, step.So, step.Zk, step.Sv, step.y00, step.gain, step.Sk,
 )
 
 
@@ -329,7 +329,6 @@
 
     counter = [0, 0, 0]
     sent = {}
-    coming = {}
     actions = {}
 
     def action(name):
@@ -339,6 +338,7 @@
         return keep
 
     groups = {}
+    freed = set()
 
     def take(which, group=None):
         if group is not None and (which, group) in groups:
@@ -354,10 +354,9 @@
             device_id=(to, y if to_y is None else to_y), device_id_type=MESH,
         )
         copy.start()
-        if send_group is None:
-            sent[name] = copy
-        else:
-            coming[name] = copy
+        sent[name] = copy
+        if send_group is not None:
+            freed.add(name)
 
     def local(name, src, dst):
         counter[2] += 1
@@ -367,8 +366,6 @@
 
     def wait_block(ref, sem):
         pltpu.make_async_copy(ref, ref, sem).wait()
-
-    freed = set()
 
     def free(*names):
         for name in names:
@@ -465,27 +462,27 @@
 
         @action(letter + "_from_s")
         def _():
-            coming[letter + "s"].wait_recv()
+            sent[letter + "s"].wait_recv()
             pass_on("sz", (1, 0, 0, 0), "z")
             pass_on("sx", (1, 0, 0, 0), "x")
             pass_on("sc", (1, 0, 0, 0), "c")
 
         @action(letter + "_from_z")
         def _():
-            coming[letter + "z"].wait_recv()
+            sent[letter + "z"].wait_recv()
             pass_on("zx", (0, 1, 0, 0), "x")
             pass_on("zc", (0, 1, 0, 0), "c")
 
         @action(letter + "_from_sz")
         def _():
-            coming[letter + "sz"].wait_recv()
+            sent[letter + "sz"].wait_recv()
             pass_on("szx", (1, 1, 0, 0), "x")
             pass_on("szc", (1, 1, 0, 0), "c")
 
         @action(letter + "_from_x")
         def _():
             for name, at in (("x", (0, 0, 1, 0)), ("sx", (1, 0, 1, 0)), ("zx", (0, 1, 1, 0)), ("szx", (1, 1, 1, 0))):
-                coming[letter + name].wait_recv()
+                sent[letter + name].wait_recv()
                 pass_on(name + "c", at, "c")
 
         @action(letter + "_from_c")
@@ -758,11 +755,11 @@
 
         @action(name + "n")
         def _():
-            link(name + "n", part(first), came.at[0, h], one)
+            link(name + "n", part(first), came.at[0, h], one, send_group=name[0])
 
         @action(name + "f")
         def _():
-            link(name + "f", part((1, 1)), came.at[1, h], one)
+            link(name + "f", part((1, 1)), came.at[1, h], one, send_group=name[0])
 
         @action(name + "t")
         def _():
@@ -772,7 +769,7 @@
             def _(m):
                 add_rows(part(second).at[m], came.at[1, h, m])
 
-            link(name + "t", part(second), came.at[2, h], two)
+            link(name + "t", part(second), came.at[2, h], two, send_group=name[0])
 
     for name, way in ROUTES.items():
         sums, came = (pg_s, pg_r) if name[0] == "p" else (po_s, po_r)
@@ -796,8 +793,8 @@
         @action("w" + tag)
         def _():
             free("gxs", "gzs", "gds")
-            if "gc" not in freed:
-                freed.add("gc")
+            if "tiles" not in freed:
+                freed.add("tiles")
                 wait_block(wgu_all.at[:, :, :, c], ssem.at[take(0, "g")])
             left = n2_all[:, :, :, :, :, pl.ds(pl.multiple_of((at[0] * 2 + at[1]) * tile, tile), tile)]
             left = left.reshape(4 * tokens, tile).T
@@ -808,7 +805,7 @@
                 part = dot(left, ggu_all[:, :, :, :, :, wide].reshape(4 * tokens, 2 * tile))
                 gu_grad[at[0], at[1], :, :, :, wide] = part.astype(bf16).reshape(2, 2, rows, 2 * tile)
 
-            link("w" + tag, gu_grad.at[at[0], at[1], :, flip(c, 1)], gu_core.at[at], peer(dc=1))
+            link("w" + tag, gu_grad.at[at[0], at[1], :, flip(c, 1)], gu_core.at[at], peer(dc=1), send_group="w")
 
         @action("y" + tag)
         def _():
@@ -945,7 +942,7 @@
                 part = dot(left[:, cols].T, right[...])
                 view(t // 2, t % 2)[...] = part.astype(bf16).reshape(2, 2, rows, width)
 
-            link("W" + letter, view(every, every, every, flip(c, 1)), attn_core.at[g], peer(dc=1))
+            link("W" + letter, view(every, every, every, flip(c, 1)), attn_core.at[g], peer(dc=1), send_group="W")
 
         @action("W" + letter)
         def _():
@@ -982,20 +979,20 @@
                 lambda m: (m // 4, (m // 2) % 2, m % 2, c),
                 lambda m: attn_core.at[g, m // 4, (m // 2) % 2, m % 2],
             )
-            link("X" + letter, view(every, every, flip(x, 1), c), attn_x.at[g], peer(dx=1))
+            link("X" + letter, view(every, every, flip(x, 1), c), attn_x.at[g], peer(dx=1), send_group="X")
 
         @action("Z" + letter)
         def _():
             sent["X" + letter].wait_recv()
             add_into(4, lambda m: (m // 2, m % 2, x, c), lambda m: attn_x.at[g, m // 2, m % 2])
-            link("Z" + letter, view(every, flip(z, 1), x, c), attn_z.at[g], peer(dz=1))
+            link("Z" + letter, view(every, flip(z, 1), x, c), attn_z.at[g], peer(dz=1), send_group="Z")
 
         @action("S" + letter)
         def _():
             sent["Z" + letter].wait_recv()
             add_into(2, lambda m: (m, z, x, c), lambda m: attn_z.at[g, m])
             cols = pl.ds(out_cols[g] * width, width)
-            link("S" + letter, view(flip(s, 1), z, x, c), attn_out.at[1, :, cols], peer(ds=1))
+            link("S" + letter, view(flip(s, 1), z, x, c), attn_out.at[1, :, cols], peer(ds=1), send_group="S", recv_group="S")
             local("keep" + letter, view(s, z, x, c), attn_out.at[0, :, cols])
 
     for letter, g in GROUPS.items():
@@ -1077,26 +1074,30 @@
     for name in ORDER:
         actions[name]()
 
-    for letter in GROUPS:
-        sent["S" + letter].wait_recv()
-        sent["keep" + letter].wait()
-    sent["dy"].wait_recv()
-    sent["dkeep"].wait()
-    wait_block(gu_grad.at[slab()], gu_sems["keep"])
-    for flips in blocks.values():
-        wait_block(wgu_all.at[slab()], ssem.at[gu_sems[flips][0]])
-        if flips[0] == 0:
-            wait_block(gu_grad.at[slab()], ssem.at[gu_sems[flips + (0,)][0]])
-            wait_block(gu_grad.at[slab()], rsem.at[gu_sems[flips + (0,)][1]])
-    sent["keep_out"].wait()
-    sent["keep_ig"].wait()
     for letter, g in GROUPS.items():
         wait_block(wa.at[g, :, :, :, c], ssem.at[take(0, letter + "c")])
         wait_block(wa.at[g, :, :, x, c], ssem.at[take(0, letter + "x")])
         wait_block(wa.at[g, :, z, x, c], ssem.at[take(0, letter + "z")])
         wait_block(wa.at[(g,) + slab()], ssem.at[take(0, letter + "s")])
-    free(*(name for name in sent if name not in ("down", "x_in", "cot_in") and not name.startswith(("keep", "dkeep"))
-           and not name.endswith("own")))
+    for flips in blocks.values():
+        wait_block(wgu_all.at[slab()], ssem.at[gu_sems[flips][0]])
+    local_only = ("down", "x_in", "cot_in")
+    free(*(name for name in sent if name not in local_only and not name.startswith(("keep", "dkeep")) and name[1:] != "own"))
+    for ref, group in ((pg_r, "p"), (po_r, "u"), (gu_core, "w"), (attn_core, "W"), (attn_x, "X"), (attn_z, "Z")):
+        wait_block(ref, ssem.at[take(0, group)])
+    sent["dy"].wait_recv()
+    sent["dkeep"].wait()
+    sent["keep_out"].wait()
+    sent["keep_ig"].wait()
+    wait_block(gu_grad.at[slab()], gu_sems["keep"])
+    for flips in blocks.values():
+        if flips[0] == 0:
+            wait_block(gu_grad.at[slab()], ssem.at[gu_sems[flips + (0,)][0]])
+            wait_block(gu_grad.at[slab()], rsem.at[gu_sems[flips + (0,)][1]])
+    for letter in GROUPS:
+        sent["keep" + letter].wait()
+    wait_block(attn_z.at[pl.ds(0, 2)], ssem.at[take(0, "S")])
+    wait_block(attn_out.at[1], rsem.at[take(1, "S")])
 
 
 def square_layer(inputs, frame_flags, attn_gain, qkv_weight, out_weight, ffn_gain, gate_up_weight, down_weight, cotangent):

time: 243 us -> 241 us (level)
  no operation moved by 1% of the time
where the time goes in v5:
time: 241 us
  Pallas kernels  240 us (100%)
    pallas_call x1, Pallas kernels, square_layer(): pl.pallas_call(square_kernel, out_shape=(jax.ShapeDtypeStruct(own, bf16),...  236 us

profile of v5, /device:TPU:0, one launch (start us, length us, event | category | flops | bytes accessed | tf_op | source)
XLA Modules:
  0.0 240.7 jit_solution(167161112288226234)
XLA Ops:
  0.6 235.6 %shard_map.152 = (bf16[256,1024]{1,0:T(8,128)(2,1)}, f32[2048,128]{1,0:T(8,128)}, f32[1,64]{1,0:T(1,128)}, f32[1,64]{1,0:T(1,128)}, bf16[64,8192]{1,0:T(8,128)(2...) custom-call(bf16[256,1024]{1,0:T(8,128)(2,1)} %bitcast.24, bf16[256,1024]{1,0:T(8,128)(2,1)} %bitcast.25, ...), custom_call_target="tpu_custom_call" | custom-call | flops 25999998976 | bytes 8388608 | tf_op jit(solution)/shard_map/pallas_call | solution.py:1173
  236.2 4.3 %shard_map.153 = (bf16[256,1024]{1,0:T(8,128)(2,1)}, f32[2048,128]{1,0:T(8,128)}, f32[64,3072]{1,0:T(8,128)}, f32[64,1024]{1,0:T(8,128)}, f32[64,8192]{1,0:T(8,1...) custom-call(bf16[256,1024]{1,0:T(8,128)(2,1)} %get-tuple-element.23.result, ...), custom_call_target="tpu_custom_call" | custom-call | tf_op jit(solution)/shard_map/pallas_call | solution.py:1206

commit v6 on v5

--- a/solution.py
+++ b/solution.py
@@ -1032,7 +1032,7 @@
                 spread = pl.ds(i * rows * (width // 128) + k, rows, width // 128)
                 ig_ref[spread, :] = grad[:, k * 128 : (k + 1) * 128]
 
-        local("keep_ig", ig_ref, ig_hbm)
+        local("keep_ig", ig_ref.at[pl.ds(0, ig_hbm.shape[0])], ig_hbm)
 
         @pl.loop(1, 16)
         def _(r):
@@ -1164,7 +1164,7 @@
         pltpu.VMEM(own, bf16),
         pltpu.VMEM(own, bf16),
         pltpu.VMEM(own, bf16),
-        pltpu.VMEM((tokens * lane_blocks, lane_block), f32),
+        pltpu.VMEM(((tokens + 1) * lane_blocks, lane_block), f32),
         pltpu.SemaphoreType.DMA((SEND_SEMS,)),
         pltpu.SemaphoreType.DMA((RECV_SEMS,)),
         pltpu.SemaphoreType.DMA((16,)),

time: 241 us -> 241 us (level)
  no operation moved by 1% of the time
where the time goes in v6:
time: 241 us
  Pallas kernels  240 us (100%)
    pallas_call x1, Pallas kernels, square_layer(): pl.pallas_call(square_kernel, out_shape=(jax.ShapeDtypeStruct(own, bf16),...  236 us

profile of v6, /device:TPU:0, one launch (start us, length us, event | category | flops | bytes accessed | tf_op | source)
XLA Modules:
  0.0 240.7 jit_solution(11857951774167391892)
XLA Ops:
  0.6 235.6 %shard_map.152 = (bf16[256,1024]{1,0:T(8,128)(2,1)}, f32[2048,128]{1,0:T(8,128)}, f32[1,64]{1,0:T(1,128)}, f32[1,64]{1,0:T(1,128)}, bf16[64,8192]{1,0:T(8,128)(2...) custom-call(bf16[256,1024]{1,0:T(8,128)(2,1)} %bitcast.24, bf16[256,1024]{1,0:T(8,128)(2,1)} %bitcast.25, ...), custom_call_target="tpu_custom_call" | custom-call | flops 25999998976 | bytes 8388608 | tf_op jit(solution)/shard_map/pallas_call | solution.py:1173
  236.3 4.3 %shard_map.153 = (bf16[256,1024]{1,0:T(8,128)(2,1)}, f32[2048,128]{1,0:T(8,128)}, f32[64,3072]{1,0:T(8,128)}, f32[64,1024]{1,0:T(8,128)}, f32[64,8192]{1,0:T(8,1...) custom-call(bf16[256,1024]{1,0:T(8,128)(2,1)} %get-tuple-element.23.result, ...), custom_call_target="tpu_custom_call" | custom-call | tf_op jit(solution)/shard_map/pallas_call | solution.py:1206

commit v7 on v6

--- a/solution.py
+++ b/solution.py
@@ -271,10 +271,10 @@
 step = Names()
 
 ORDER = (
-    step.v_to_c, step.k_to_x, step.mask, step.k_to_z, step.k_to_c, step.v_to_x, step.o_to_z, step.k_to_s,
-    step.v_to_s, step.q_to_s, step.o_to_c, step.gx, step.k_from_s, step.q_to_c, step.v_to_z, step.q_to_x,
-    step.o_to_s, step.k_from_sz, step.k_from_z, step.v_from_s, step.q_to_z, step.v_from_sz, step.o_from_s,
-    step.norm, step.gz, step.q_from_z, step.v_from_z, step.gs, step.q_from_s, step.v_from_x, step.v_from_c,
+    step.v_to_c, step.mask, step.k_to_x, step.k_to_z, step.k_to_c, step.v_to_x, step.o_to_z, step.k_to_s,
+    step.v_to_s, step.q_to_s, step.o_to_c, step.norm, step.gx, step.k_from_s, step.q_to_c, step.v_to_z,
+    step.q_to_x, step.o_to_s, step.k_from_sz, step.k_from_z, step.v_from_s, step.q_to_z, step.v_from_sz,
+    step.o_from_s, step.gz, step.q_from_z, step.v_from_z, step.gs, step.q_from_s, step.v_from_x, step.v_from_c,
     step.ends, step.gz_from, step.d_to, step.k_from_x, step.gd, step.v_rows, step.q_from_sz, step.cz, step.o_to_x,
     step.cx, step.g_own, step.q_from_x, step.o_from_z, step.o_from_sz, step.g_own_from, step.q_from_c,
     step.k_from_c, step.gx_from, step.k_rows, step.q_rows, step.gzs_from, step.attn, step.o_from_x, step.o_from_c,

time: 241 us -> 241 us (level)
  no operation moved by 1% of the time
where the time goes in v7:
time: 241 us
  Pallas kernels  240 us (100%)
    pallas_call x1, Pallas kernels, square_layer(): pl.pallas_call(square_kernel, out_shape=(jax.ShapeDtypeStruct(own, bf16),...  236 us

profile of v7, /device:TPU:0, one launch (start us, length us, event | category | flops | bytes accessed | tf_op | source)
XLA Modules:
  0.0 240.7 jit_solution(4724437635967666050)
XLA Ops:
  0.6 235.5 %shard_map.152 = (bf16[256,1024]{1,0:T(8,128)(2,1)}, f32[2048,128]{1,0:T(8,128)}, f32[1,64]{1,0:T(1,128)}, f32[1,64]{1,0:T(1,128)}, bf16[64,8192]{1,0:T(8,128)(2...) custom-call(bf16[256,1024]{1,0:T(8,128)(2,1)} %bitcast.24, bf16[256,1024]{1,0:T(8,128)(2,1)} %bitcast.25, ...), custom_call_target="tpu_custom_call" | custom-call | flops 25999998976 | bytes 8388608 | tf_op jit(solution)/shard_map/pallas_call | solution.py:1173
  236.2 4.3 %shard_map.153 = (bf16[256,1024]{1,0:T(8,128)(2,1)}, f32[2048,128]{1,0:T(8,128)}, f32[64,3072]{1,0:T(8,128)}, f32[64,1024]{1,0:T(8,128)}, f32[64,8192]{1,0:T(8,1...) custom-call(bf16[256,1024]{1,0:T(8,128)(2,1)} %get-tuple-element.23.result, ...), custom_call_target="tpu_custom_call" | custom-call | tf_op jit(solution)/shard_map/pallas_call | solution.py:1206
